TPU v7x, 32 devices: a whole 2x2x4 slice. The times are simulated.
32 devices in a mesh: ctx: 8 (over z, y), tp: 4 (over x, core).
Axes of the slice: x: 2, y: 2, z: 4, core: 2. Of those that a mesh axis runs over, the one named last changes fastest.
Arguments:
- hidden: bfloat16 [2048, 2048], P('ctx', 'tp'), may hold values from -6 to 6
- norm_gain_a: float32 [2048], replicated, may hold values from 0.5 to 1.5
- in_weight_a: bfloat16 [3, 2048, 2048], P(None, 'ctx', 'tp'), may hold values from -0.125 to 0.125
- mr_filter: bfloat16 [128, 128], P('tp'), may hold values from -0.5 to 0.5
- out_weight_a: bfloat16 [2048, 2048], P('tp', 'ctx'), may hold values from -0.125 to 0.125
- norm_gain_b: float32 [2048], replicated, may hold values from 0.5 to 1.5
- in_weight_b: bfloat16 [3, 2048, 2048], P(None, 'ctx', 'tp'), may hold values from -0.125 to 0.125
- li_rate: float32 [128, 16], P('tp'), may hold values from 4.8828125e-05 to 0.0333333333
- li_residue: float32 [128, 16], P('tp'), may hold values from -3 to 3
- out_weight_b: bfloat16 [2048, 2048], P('tp', 'ctx'), may hold values from -0.125 to 0.125
Outputs:
- mixed: bfloat16 [2048, 2048], P('ctx', 'tp')
- gated_medium: bfloat16 [2048, 2048], P('tp', 'ctx')
- gated_long: bfloat16 [2048, 2048], P('tp', 'ctx')
All inputs are finite; a program needn't handle non-finite values.
Results may differ from a plain program's by a relative error of at most 0.02.
Values may be sent and summed in bfloat16 or wider, within the bound.
A program may use at most 64 MiB of HBM per device.

v0:
```python
import jax
import jax.numpy as jnp
from jax import lax
from jax.sharding import PartitionSpec as P

GROUP = 16
TAPS = 128


highest = lax.Precision.HIGHEST


def passed_along(value, axis, steps):
    count = lax.axis_size(axis)
    initial, last = (max(0, -steps), min(count, count - steps))
    return lax.ppermute(value, axis, [(source, source + steps) for source in range(initial, last)])


def normalize(values, gain):
    widened = values.astype(jnp.float32)
    factor = lax.rsqrt(jnp.mean(widened * widened, axis=1, keepdims=True) + 1e-06)
    return (widened * factor * gain).astype(jnp.bfloat16)


def layer_inputs(gathered, gain, weight):
    normed = normalize(gathered, gain)
    projected = jnp.einsum(
        "knc,tn->kct",
        lax.all_gather(weight, "ctx", axis=1, tiled=True),
        normed,
        preferred_element_type=jnp.float32,
    )
    return (projected[1], (projected[0] * projected[2]).astype(jnp.bfloat16))


def out_project(gated, weight):
    return jnp.einsum(
        "ct,cn->tn",
        gated,
        lax.all_gather(weight, "ctx", axis=1, tiled=True),
        preferred_element_type=jnp.float32,
    )


def toeplitz_rows(filters):
    group_count, tap_count = filters.shape
    padded_filter = jnp.concatenate(
        [
            jnp.zeros((group_count, 1), filters.dtype),
            filters[:, ::-1],
            jnp.zeros((group_count, tap_count), filters.dtype),
        ],
        axis=1,
    )
    tiled = jnp.tile(padded_filter, (1, tap_count))[:, : tap_count * 2 * tap_count]
    return tiled.reshape(group_count, tap_count, 2 * tap_count)


def medium_conv(medium_in, mr_filter):
    channels_here, tokens_here = medium_in.shape
    prior_rim = passed_along(medium_in[:, tokens_here - TAPS :], "ctx", 1)
    extended = jnp.concatenate([prior_rim, medium_in], axis=1)
    group_count = channels_here // GROUP
    block_count = tokens_here // TAPS
    grouped = extended.reshape(group_count, GROUP, block_count + 1, TAPS)
    windows = jnp.concatenate([grouped[:, :, :-1], grouped[:, :, 1:]], axis=3)
    filter_rows = toeplitz_rows(mr_filter)
    result = jnp.einsum("gts,gkbs->gkbt", filter_rows, windows, preferred_element_type=jnp.float32)
    return result.reshape(channels_here, tokens_here)


def chain_blocks(earlier, latter):
    return (earlier[0] * latter[1] + latter[0], earlier[1] * latter[1])


def long_parts(values, decay_rates, residues):
    group_count, per_group, length = values.shape
    block_count = length // TAPS
    blocks = values.astype(jnp.float32).reshape(group_count, per_group, block_count, TAPS)
    offsets = jnp.arange(TAPS, dtype=jnp.float32)
    mode_weight = residues * jnp.sqrt(2.0 * decay_rates)
    impulse = jnp.einsum(
        "gm,gmt->gt", mode_weight, jnp.exp(-decay_rates[:, :, None] * offsets), precision=highest
    )
    within_rows = toeplitz_rows(impulse)[:, :, TAPS:]
    within = jnp.einsum("gts,gkbs->gkbt", within_rows, blocks, precision=highest)
    to_end = jnp.exp(-decay_rates[:, :, None] * (TAPS - 1.0 - offsets))
    block_end = jnp.einsum("gms,gkbs->gkbm", to_end, blocks, precision=highest)
    block_decay = jnp.broadcast_to(jnp.exp(-decay_rates * TAPS)[:, None, None, :], block_end.shape)
    after_block, unused_decay = lax.associative_scan(chain_blocks, (block_end, block_decay), axis=2)
    entering = jnp.concatenate(
        [jnp.zeros_like(after_block[:, :, :1]), after_block[:, :, :-1]], axis=2
    )
    from_start = mode_weight[:, :, None] * jnp.exp(-decay_rates[:, :, None] * (offsets + 1.0))
    carried = jnp.einsum("gmt,gkbm->gkbt", from_start, entering, precision=highest)
    return ((within + carried).reshape(group_count, per_group, length), after_block[:, :, -1])


def per_device(
    hidden,
    norm_gain_a,
    in_weight_a,
    mr_filter,
    out_weight_a,
    norm_gain_b,
    in_weight_b,
    li_rate,
    li_residue,
    out_weight_b,
):
    gathered = lax.all_gather(hidden, "tp", axis=1, tiled=True)
    first_gate, medium_in = layer_inputs(gathered, norm_gain_a, in_weight_a)
    medium = medium_conv(medium_in, mr_filter)
    gated_medium = (first_gate * medium).astype(jnp.bfloat16)
    first_partial = out_project(gated_medium, out_weight_a)
    first_summed = lax.psum_scatter(
        first_partial.astype(jnp.bfloat16), "tp", scatter_dimension=1, tiled=True
    ).astype(jnp.float32)
    after_a = (hidden.astype(jnp.float32) + first_summed).astype(jnp.bfloat16)
    gathered_next = lax.all_gather(after_a, "tp", axis=1, tiled=True)
    second_gate, long_in = layer_inputs(gathered_next, norm_gain_b, in_weight_b)
    by_channel = lax.all_to_all(long_in, "ctx", split_axis=0, concat_axis=1, tiled=True)
    channel_count, full_length = by_channel.shape
    groups_here = max(1, channel_count // GROUP)
    per_group = channel_count // groups_here
    first_group = lax.axis_index("ctx") * channel_count // GROUP
    rates_here = lax.dynamic_slice_in_dim(li_rate, first_group, groups_here, 0)
    residues_here = lax.dynamic_slice_in_dim(li_residue, first_group, groups_here, 0)
    long_whole, unused_end = long_parts(
        by_channel.reshape(groups_here, per_group, full_length), rates_here, residues_here
    )
    long_out = lax.all_to_all(
        long_whole.reshape(channel_count, full_length).astype(jnp.bfloat16),
        "ctx",
        split_axis=1,
        concat_axis=0,
        tiled=True,
    ).astype(jnp.float32)
    gated_long = (second_gate * long_out).astype(jnp.bfloat16)
    second_partial = out_project(gated_long, out_weight_b)
    second_summed = lax.psum_scatter(
        second_partial.astype(jnp.bfloat16), "tp", scatter_dimension=1, tiled=True
    ).astype(jnp.float32)
    mixed = (after_a.astype(jnp.float32) + second_summed).astype(jnp.bfloat16)
    return (mixed, gated_medium, gated_long)


def solution(mesh):
    in_specs = (
        P("ctx", "tp"),
        P(),
        P(None, "ctx", "tp"),
        P("tp", None),
        P("tp", "ctx"),
        P(),
        P(None, "ctx", "tp"),
        P("tp", None),
        P("tp", None),
        P("tp", "ctx"),
    )
    out_specs = (P("ctx", "tp"), P("tp", "ctx"), P("tp", "ctx"))
    return jax.shard_map(
        per_device, mesh=mesh, in_specs=in_specs, out_specs=out_specs, check_vma=False
    )
```

profile of v0, /device:TPU:0, one launch (start us, length us, event | category | flops | bytes accessed | tf_op | source)
XLA Modules:
  0.0 425.5 jit_solution(15276197137684297743)
XLA Ops:
  10.3 18.7 %all-gather.7.cloned.1.call-done = bf16[256,2048]{1,0:T(8,128)(2,1)} async-done(((bf16[256,512]{1,0:T(8,128)(2,1)}), bf16[256,2048]{1,0:T(8,128)(2,1)}) %all-gather.7.cloned.1.call-update) | async-done | bytes 1048592 | tf_op jit(solution)/shard_map/all_gather | solution.py:111
  29.0 1.5 fusion
  30.6 99.7 %all-gather.9.cloned.1.call-done = bf16[3,2048,512]{2,1,0:T(8,128)(2,1)} async-done(((bf16[3,256,512]{2,1,0:T(8,128)(2,1)}), bf16[3,2048,512]{2,1,0:T(8,128)(2,1)}) %all-gather.9.cloned.1.call-update) | async-done | bytes 6291472 | tf_op jit(solution)/shard_map/all_gather | solution.py:29
  130.3 5.0 %convolution_bitcast_fusion.1 = f32[3,512,256]{1,2,0:T(8,128)S(1)} fusion(bf16[3,2048,512]{2,1,0:T(8,128)(2,1)} %all-gather.9.cloned.1.call-done, bf16[256,2048]{1,0:T(8,128)(2,1)} %all-gather.7.cloned.1.call-done, f32[2048]{0:T(1024)S(1)} %copy-done.5, f32[256]{0:T(256)S(1)} %add_rsqrt_fusion.1), kind=kOutput, calls=%fused_computation.15 | convolution fusion | flops 1612709888 | bytes 8922112 | tf_op jit(solution)/shard_map/knc,tn->kct/dot_general | solution.py:27
  135.4 3.1 collective-permute-start
  138.8 4.4 %tile.9 = bf16[32,32896]{1,0:T(8,128)(2,1)} reshape(bf16[32,128,257]{2,1,0:T(8,128)(2,1)S(1)} %tile.8) | data formatting | bytes 4210688 | tf_op jit(solution)/shard_map/tile | solution.py:55
  143.3 1.6 slice-done
  145.4 0.9 pad_maximum_fusion
  148.5 1.1 fusion.22
  149.6 32.6 %all-gather.11.cloned.1.call-done = bf16[512,2048]{1,0:T(8,128)(2,1)} async-done(((bf16[512,256]{1,0:T(8,128)(2,1)}), bf16[512,2048]{1,0:T(8,128)(2,1)}) %all-gather.11.cloned.1.call-update) | async-done | bytes 2097168 | tf_op jit(solution)/shard_map/all_gather | solution.py:40
  182.1 3.3 convolution_convert_fusion.1
  185.5 23.2 %reduce-scatter.3.cloned.1.call-done = bf16[256,512]{1,0:T(8,128)(2,1)} async-done(((bf16[256,2048]{1,0:T(8,128)(2,1)}), bf16[256,512]{1,0:T(8,128)(2,1)}) %reduce-scatter.3.cloned.1.call-update) | async-done | bytes 262160 | tf_op jit(solution)/shard_map/reduce_scatter | solution.py:116
  208.7 1.7 add_convert_fusion.1
  212.1 15.5 %all-gather.13.cloned.1.call-done = bf16[256,2048]{1,0:T(8,128)(2,1)} async-done(((bf16[256,512]{1,0:T(8,128)(2,1)}), bf16[256,2048]{1,0:T(8,128)(2,1)}) %all-gather.13.cloned.1.call-update) | async-done | bytes 1048592 | tf_op jit(solution)/shard_map/all_gather | solution.py:120
  227.5 1.5 fusion.3
  229.0 99.8 %all-gather.15.cloned.1.call-done = bf16[3,2048,512]{2,1,0:T(8,128)(2,1)} async-done(((bf16[3,256,512]{2,1,0:T(8,128)(2,1)}), bf16[3,2048,512]{2,1,0:T(8,128)(2,1)}) %all-gather.15.cloned.1.call-update) | async-done | bytes 6291472 | tf_op jit(solution)/shard_map/all_gather | solution.py:29
  328.9 5.0 %convolution_bitcast_fusion = f32[3,512,256]{1,2,0:T(8,128)S(1)} fusion(bf16[3,2048,512]{2,1,0:T(8,128)(2,1)} %all-gather.15.cloned.1.call-done, bf16[256,2048]{1,0:T(8,128)(2,1)} %all-gather.13.cloned.1.call-done, f32[2048]{0:T(1024)S(1)} %copy-done.6, f32[256]{0:T(256)S(1)} %add_rsqrt_fusion), kind=kOutput, calls=%fused_computation.14 | convolution fusion | flops 1612709888 | bytes 8922112 | tf_op jit(solution)/shard_map/knc,tn->kct/dot_general | solution.py:27
  333.9 0.8 copy.54
  334.8 3.4 all-to-all-start
  339.7 0.9 copy.77
  340.7 10.9 %all-to-all-done = bf16[8,64,256]{2,1,0:T(8,128)(2,1)S(1)} async-done(((bf16[8,64,256]{2,1,0:T(8,128)(2,1)}), bf16[8,64,256]{2,1,0:T(8,128)(2,1)S(1)}, u32[]{:S(2)}, u32[]{:S(2)}) %all-to-all-start) | async-done | bytes 262176 | tf_op jit(solution)/shard_map/all_to_all | solution.py:122
  353.6 1.4 slice.153
  355.2 0.9 pad.29
  356.2 0.9 pad.28
  359.0 1.0 fusion.28
  360.6 1.3 fusion.29
  362.9 18.6 %all_to_all.23 = bf16[64,8,256]{2,0,1:T(8,128)(2,1)S(1)} all-to-all(bf16[64,8,256]{2,0,1:T(8,128)(2,1)S(1)} %copy.58), channel_id=1, replica_groups=mesh['ctx'=8,'tp'=4] {'ctx'}, dimensions={1} | all-to-all | bytes 524288 | tf_op jit(solution)/shard_map/all_to_all | solution.py:132
  381.8 5.9 %all-gather.17.cloned.1.call-done = bf16[512,2048]{1,0:T(8,128)(2,1)} async-done(((bf16[512,256]{1,0:T(8,128)(2,1)}), bf16[512,2048]{1,0:T(8,128)(2,1)}) %all-gather.17.cloned.1.call-update) | async-done | bytes 2097168 | tf_op jit(solution)/shard_map/all_gather | solution.py:40
  387.7 3.3 convolution_convert_fusion
  391.1 0.8 copy.60
  392.7 24.2 %reduce-scatter.5.cloned.1.call-done = bf16[256,512]{1,0:T(8,128)(2,1)} async-done(((bf16[256,2048]{1,0:T(8,128)(2,1)}), bf16[256,512]{1,0:T(8,128)(2,1)}) %reduce-scatter.5.cloned.1.call-update) | async-done | bytes 262160 | tf_op jit(solution)/shard_map/reduce_scatter | solution.py:141
  417.0 1.7 add_convert_fusion
  (104 shorter events, 16.3 us)
Async XLA Ops:
  7.2 123.1 %copy-start.5 = (f32[2048]{0:T(1024)S(1)}, f32[2048]{0:T(1024)}, u32[]{:S(2)}) copy-start(f32[2048]{0:T(1024)} %param.11) | copy-start | bytes 24580
  7.2 21.9 %all-gather.7.cloned.1.call-start = ((), (), s32[]{:S(2)}) async-start(), calls=%async_computation.4 | async-start | bytes 1310720 | tf_op jit(solution)/shard_map/all_gather | solution.py:111
  7.9 122.4 %all-gather.9.cloned.1.call-start = ((), (), s32[]{:S(2)}) async-start(), calls=%async_computation.5 | async-start | bytes 7077888 | tf_op jit(solution)/shard_map/all_gather | solution.py:29
  8.7 173.5 %all-gather.11.cloned.1.call-start = ((), (), s32[]{:S(2)}) async-start(), calls=%async_computation.6 | async-start | bytes 2359296 | tf_op jit(solution)/shard_map/all_gather | solution.py:40
  9.4 199.3 %reduce-scatter.3.cloned.1.call-start = ((), (), s32[]{:S(2)}) async-start(), calls=%async_computation.7 | async-start | bytes 1310720 | tf_op jit(solution)/shard_map/reduce_scatter | solution.py:116
  135.3 3.2 copy-start.1
  135.4 10.0 %collective-permute-start = (bf16[512,128]{0,1:T(8,128)(2,1)S(1)}, bf16[512,128]{0,1:T(8,128)(2,1)}, u32[]{:S(2)}, u32[]{:S(2)}) collective-permute-start(bf16[512,128]{0,1:T(8,128)(2,1)S(1)} %slice.158), channel_id=1, source_target_pairs={{0,4},{4,8},{8,12},{12,16},{16,20},{20,24},{24,28},{1,5},{5,9},{9,... | collective-permute-start | bytes 393224 | tf_op jit(solution)/shard_map/ppermute | solution.py:16
  143.3 1.6 slice-start
  149.6 59.1 %copy-start.2 = (bf16[256,512]{1,0:T(8,128)(2,1)S(1)}, bf16[256,512]{1,0:T(8,128)(2,1)}, u32[]{:S(2)}) copy-start(bf16[256,512]{1,0:T(8,128)(2,1)} %param.10) | copy-start | bytes 786436
  185.4 26.4 %copy-start.3 = (f32[32,16]{0,1:T(8,128)S(1)}, f32[32,16]{0,1:T(8,128)}, u32[]{:S(2)}) copy-start(f32[32,16]{0,1:T(8,128)} %param.17) | copy-start | bytes 6148
  185.4 26.4 %copy-start.4 = (f32[32,16]{0,1:T(8,128)S(1)}, f32[32,16]{0,1:T(8,128)}, u32[]{:S(2)}) copy-start(f32[32,16]{0,1:T(8,128)} %param.18) | copy-start | bytes 6148
  185.4 143.4 %copy-start.6 = (f32[2048]{0:T(1024)S(1)}, f32[2048]{0:T(1024)}, u32[]{:S(2)}) copy-start(f32[2048]{0:T(1024)} %param.15) | copy-start | bytes 24580
  185.5 42.1 %all-gather.13.cloned.1.call-start = ((), (), s32[]{:S(2)}) async-start(), calls=%async_computation.8 | async-start | bytes 1310720 | tf_op jit(solution)/shard_map/all_gather | solution.py:120
  210.4 118.4 %all-gather.15.cloned.1.call-start = ((), (), s32[]{:S(2)}) async-start(), calls=%async_computation.9 | async-start | bytes 7077888 | tf_op jit(solution)/shard_map/all_gather | solution.py:29
  211.0 176.7 %all-gather.17.cloned.1.call-start = ((), (), s32[]{:S(2)}) async-start(), calls=%async_computation.10 | async-start | bytes 2359296 | tf_op jit(solution)/shard_map/all_gather | solution.py:40
  334.8 16.8 %all-to-all-start = ((bf16[8,64,256]{2,1,0:T(8,128)(2,1)}), bf16[8,64,256]{2,1,0:T(8,128)(2,1)S(1)}, u32[]{:S(2)}, u32[]{:S(2)}) async-start(bf16[8,64,256]{2,1,0:T(8,128)(2,1)} %bitcast.8), calls=%async_computation.1 | async-start | bytes 524288 | tf_op jit(solution)/shard_map/all_to_all | solution.py:122
  338.2 78.8 %reduce-scatter.5.cloned.1.call-start = ((), (), s32[]{:S(2)}) async-start(), calls=%async_computation.11 | async-start | bytes 1310720 | tf_op jit(solution)/shard_map/reduce_scatter | solution.py:141
  381.8 35.2 %copy-start = (bf16[256,512]{1,0:T(8,128)(2,1)S(1)}, bf16[256,512]{1,0:T(8,128)(2,1)}, u32[]{:S(2)}) copy-start(bf16[256,512]{1,0:T(8,128)(2,1)} %add_convert_fusion.1) | copy-start | bytes 786436
Sparse Core Ops, SparseCore 0:
  9.6 19.4 all-gather.6
  31.2 99.0 all-gather.8
  132.3 49.7 all-gather.10
  185.6 23.0 reduce-scatter.2
  210.8 16.7 all-gather.12
  229.8 99.0 all-gather.14
  331.1 56.5 all-gather.16
  391.2 25.7 reduce-scatter.4
where the time goes:
time: 426 us
  waiting for transfers between devices  334 us (78%)
  local copies, waits for them, and re-layouts  20.7 us (5%)
  matrix products  20 us (5%)
  blocking collectives  18.6 us (4%)
  between operations  14.6 us (3%)
  other arithmetic  10.8 us (3%)
  starting transfers between devices  7.02 us (2%)
    all_gather x2, waiting for transfers between devices, layer_inputs(): lax.all_gather(weight, 'ctx', axis=1, tiled=True)  200 us
    all_gather x2, waiting for transfers between devices, out_project(): lax.all_gather(weight, 'ctx', axis=1, tiled=True)  38.5 us
    reduce_scatter x1, waiting for transfers between devices, per_device(): lax.psum_scatter(second_partial.astype(jnp.bfloat16), 'tp', scatter_dimen...  24.2 us
    reduce_scatter x1, waiting for transfers between devices, per_device(): lax.psum_scatter(first_partial.astype(jnp.bfloat16), 'tp', scatter_dimens...  23.2 us
    all_gather x1, waiting for transfers between devices, per_device(): gathered = lax.all_gather(hidden, 'tp', axis=1, tiled=True)  18.7 us
    all_to_all x1, blocking collectives, per_device(): lax.all_to_all(long_whole.reshape(channel_count, full_length).astype(jnp....  18.6 us
    all_gather x1, waiting for transfers between devices, per_device(): gathered_next = lax.all_gather(after_a, 'tp', axis=1, tiled=True)  15.5 us
    all_to_all x1, waiting for transfers between devices, per_device(): lax.all_to_all(long_in, 'ctx', split_axis=0, concat_axis=1, tiled=True)  10.9 us
  transfers between devices with their start and end apart: 10, of which 9 were waited for; matrix products, arithmetic and copies ran while one was open for 9% of the time, Pallas kernels for 0%

commit v1 on v0

v1 whole, which is shorter than its diff:
```python
import functools

import jax
import jax.numpy as jnp
from jax import lax
from jax.experimental import pallas as pl
from jax.experimental.pallas import tpu as pltpu
from jax.sharding import PartitionSpec as P

LANES = 128
MESH = pl.DeviceIdType.MESH
f32 = jnp.float32
bf16 = jnp.bfloat16
highest = lax.Precision.HIGHEST


def dot(a, b, precision=None):
    return lax.dot_general(
        a, b, (((1,), (0,)), ((), ())), precision=precision, preferred_element_type=f32
    )


def iota(shape, dim):
    return lax.broadcasted_iota(jnp.int32, shape, dim)


def kernel(
    n,
    ntp,
    hidden,
    gain_a,
    win_a,
    mr_filter,
    wout_a,
    gain_b,
    win_b,
    rate,
    residue,
    mode_rows,
    rate_mc,
    wout_b,
    mixed,
    gated_a_out,
    gated_b_out,
    wa,
    oa,
    wb,
    ob,
    hbuf,
    abuf,
    normed,
    proj,
    xin,
    halo,
    conv,
    gated,
    part,
    landed,
    states,
    toep_a,
    toep_b,
    rows_a,
    rows_b,
    to_end,
    from_start,
    ring_send,
    ring_recv,
    tp_send,
    tp_recv,
    state_send,
    state_recv,
    halo_sems,
    local_sems,
):
    me = lax.axis_index("ctx")
    mytp = lax.axis_index("tp")
    tokens, width = hidden.shape
    channels = win_a.shape[2]
    dn = win_a.shape[1]
    on = wout_a.shape[1]
    features = width * ntp
    groups, taps = mr_filter.shape
    modes = rate.shape[1]
    per = channels // groups
    tile_groups = LANES // per
    tiles = channels // LANES
    blocks = tokens // taps
    half_ring = n // 2

    odd = lax.rem(me, 2)
    pos = (1 - odd) * lax.div(me, 2) + odd * (n - 1 - lax.div(me, 2))

    def index_at(position):
        p = lax.rem(position + 2 * n, n)
        back = lax.div(p, half_ring)
        return (1 - back) * (2 * p) + back * (2 * (n - 1 - p) + 1)

    neighbour = (index_at(pos + 1), index_at(pos - 1))

    barrier = pltpu.get_barrier_semaphore()

    def greet_ctx(off, carry):
        pl.semaphore_signal(
            barrier, inc=1, device_id={"ctx": lax.rem(me + off, n)}, device_id_type=MESH
        )
        return carry

    lax.fori_loop(1, n, greet_ctx, 0)
    for off in range(1, ntp):
        pl.semaphore_signal(
            barrier, inc=1, device_id={"tp": lax.rem(mytp + off, ntp)}, device_id_type=MESH
        )

    def in_rows(ref, owner, way):
        half = dn // 2
        return ref.at[:, pl.ds(pl.multiple_of(owner * dn + way * half, half), half), :]

    def out_rows(ref, owner, way):
        half = channels // 2
        return ref.at[owner, pl.ds(way * half, half), :]

    streams = (
        (win_a, wa, in_rows, lambda way: win_a.at[:, pl.ds(way * (dn // 2), dn // 2), :]),
        (wout_a, oa, out_rows, lambda way: wout_a.at[pl.ds(way * (channels // 2), channels // 2), :]),
        (win_b, wb, in_rows, lambda way: win_b.at[:, pl.ds(way * (dn // 2), dn // 2), :]),
        (wout_b, ob, out_rows, lambda way: wout_b.at[pl.ds(way * (channels // 2), channels // 2), :]),
    )

    def ring_copy(stream, way, step, first=False):
        source, buffer, rows, own = streams[stream]
        owner = index_at(pos - step) if way == 0 else index_at(pos + step)
        return pltpu.make_async_remote_copy(
            src_ref=own(way) if first else rows(buffer, owner, way),
            dst_ref=rows(buffer, owner, way),
            send_sem=ring_send.at[stream, way, step],
            recv_sem=ring_recv.at[stream, way, step],
            device_id={"ctx": neighbour[way]},
            device_id_type=MESH,
        )

    def arrival(stream, way, step):
        source, buffer, rows, own = streams[stream]
        owner = index_at(pos - step - 1) if way == 0 else index_at(pos + step + 1)
        return pltpu.make_async_remote_copy(
            src_ref=rows(buffer, owner, way),
            dst_ref=rows(buffer, owner, way),
            send_sem=ring_send.at[stream, way, step],
            recv_sem=ring_recv.at[stream, way, step],
            device_id={"ctx": neighbour[way]},
            device_id_type=MESH,
        )

    def ring_start(stream):
        for way in (0, 1):
            ring_copy(stream, way, 0, True).start()

    def pump(which, low, high):
        def body(step, carry):
            for stream in which:
                for way in (0, 1):
                    arrival(stream, way, step - 1).wait_recv()
                    ring_copy(stream, way, step).start()
            return carry

        if high > low:
            lax.fori_loop(low, high, body, 0)

    def ring_end(stream):
        for way in (0, 1):
            arrival(stream, way, n - 2).wait_recv()

    def own_copy(stream):
        if stream in (0, 2):
            source, buffer = streams[stream][:2]
            target = buffer.at[:, pl.ds(pl.multiple_of(me * dn, dn), dn), :]
        else:
            source, buffer = streams[stream][:2]
            target = buffer.at[me]
        return pltpu.make_async_copy(source, target, local_sems.at[stream])

    def tp_copy(use, off, src, dst):
        return pltpu.make_async_remote_copy(
            src_ref=src,
            dst_ref=dst,
            send_sem=tp_send.at[use, off - 1],
            recv_sem=tp_recv.at[use, off - 1],
            device_id={"tp": lax.rem(mytp + off, ntp)},
            device_id_type=MESH,
        )

    def gather_start(use, buffer):
        for off in range(1, ntp):
            tp_copy(use, off, buffer.at[mytp], buffer.at[mytp]).start()

    def gather_wait(use, buffer):
        for off in range(1, ntp):
            sender = lax.rem(mytp - off + ntp, ntp)
            tp_copy(use, off, buffer.at[sender], buffer.at[sender]).wait_recv()

    def gather_sent(use, buffer):
        for off in range(1, ntp):
            tp_copy(use, off, buffer.at[mytp], buffer.at[mytp]).wait_send()

    def normalize(buffer, gain):
        total = jnp.zeros((tokens, 1), f32)
        for block in range(ntp):
            wide = buffer[block].astype(f32)
            total = total + jnp.sum(wide * wide, axis=1, keepdims=True)
        factor = lax.rsqrt(total / features + 1e-06)
        for block in range(ntp):
            at = slice(block * width, (block + 1) * width)
            normed[:, at] = (buffer[block].astype(f32) * factor * gain[:, at]).astype(bf16)

    def in_project(weight):
        span = min(256, channels)

        def body(k, carry):
            for at in range(0, channels, span):
                proj[k, :, at : at + span] = dot(normed[...], weight[k, :, at : at + span])
            return carry

        lax.fori_loop(0, 3, body, 0)
        xin[...] = (proj[0] * proj[2]).astype(bf16)

    def out_block(buffer, p, j):
        return dot(gated[...], buffer[p * (width // on) + j])

    def scatter_start(which, use, buffer):
        for off in range(1, ntp):
            p = lax.rem(mytp + off, ntp)
            for j in range(width // on):
                part[which, off - 1, :, j * on : (j + 1) * on] = out_block(buffer, p, j).astype(bf16)
            tp_copy(use, off, part.at[which, off - 1], landed.at[which, off - 1]).start()
        for j in range(width // on):
            proj[0, :, j * on : (j + 1) * on] = out_block(buffer, mytp, j)

    def scatter_end(which, use, base):
        total = base.astype(f32) + proj[0, :, :width]
        for off in range(1, ntp):
            tp_copy(use, off, part.at[which, off - 1], landed.at[which, off - 1]).wait_recv()
            total = total + landed[which, off - 1].astype(f32)
        return total.astype(bf16)

    def scatter_sent(which, use):
        for off in range(1, ntp):
            tp_copy(use, off, part.at[which, off - 1], landed.at[which, off - 1]).wait_send()

    def lanes(q):
        return pl.ds(pl.multiple_of(q * LANES, LANES), LANES)

    hbuf[mytp] = hidden[...]
    for stream in range(4):
        own_copy(stream).start()
    pl.semaphore_wait(barrier, (n - 1) + (ntp - 1))

    gather_start(0, hbuf)
    ring_start(0)
    ring_start(1)

    flip = (lax.rem(iota((taps, taps), 0) + iota((taps, taps), 1), taps) == 0).astype(bf16)
    rows_a[...] = dot(mr_filter[...], flip)
    lag = lax.rem(tokens - iota((groups, tokens), 1), tokens).astype(f32)
    impulse = jnp.zeros((groups, tokens), f32)
    for m in range(modes):
        r = rate[:, m : m + 1]
        impulse = impulse + residue[:, m : m + 1] * jnp.sqrt(2.0 * r) * jnp.exp(-r * lag)
    rows_b[...] = impulse

    def build(g, carry):
        row = jnp.broadcast_to(rows_a[pl.ds(g, 1), :], (taps, taps))
        turned = pltpu.roll(row, 0, 1, stride=1, stride_axis=0)
        below = iota((taps, taps), 1) <= iota((taps, taps), 0)
        toep_a[g, :, :taps] = jnp.where(below, 0.0, turned).astype(bf16)
        toep_a[g, :, taps:] = jnp.where(below, turned, 0.0).astype(bf16)
        row = jnp.broadcast_to(rows_b[pl.ds(g, 1), :], (tokens, tokens))
        turned = pltpu.roll(row, 0, 1, stride=1, stride_axis=0)
        below = iota((tokens, tokens), 1) <= iota((tokens, tokens), 0)
        toep_b[g] = jnp.where(below, turned, 0.0).astype(bf16)
        return carry

    lax.fori_loop(0, groups, build, 0)
    pump((0, 1), 1, min(2, n - 1))

    rate_row = mode_rows[0:1, :]
    weight_row = mode_rows[1:2, :] * jnp.sqrt(2.0 * rate_row)
    position = iota((tokens, groups * modes), 0).astype(f32)
    from_start[...] = weight_row * jnp.exp(-rate_row * (position + 1.0))
    to_end[...] = jnp.exp(-rate_row * (tokens - 1.0 - position)).T

    gather_wait(0, hbuf)
    normalize(hbuf, gain_a)
    pump((0, 1), 2, n - 1)
    own_copy(0).wait()
    own_copy(1).wait()
    ring_start(2)
    ring_start(3)
    ring_end(0)

    in_project(wa)
    onward = pltpu.make_async_remote_copy(
        src_ref=xin.at[pl.ds(tokens - taps, taps), :],
        dst_ref=halo,
        send_sem=halo_sems.at[0],
        recv_sem=halo_sems.at[1],
        device_id={"ctx": lax.rem(me + 1, n)},
        device_id_type=MESH,
    )
    onward.start()
    ring_end(1)
    steps = [1 + (n - 2) * k // 4 for k in range(5)]
    pump((2, 3), steps[0], steps[1])
    onward.wait()

    def medium_tile(q, carry):
        at = lanes(q)
        before = halo[:, at]
        before = jnp.where(me > 0, before, jnp.zeros_like(before))
        here = [xin[b * taps : (b + 1) * taps, at] for b in range(blocks)]
        early = [before] + here[:-1]
        window = jnp.concatenate(
            [jnp.concatenate(early, axis=1), jnp.concatenate(here, axis=1)], axis=0
        )
        group_of = lax.div(lax.rem(iota((taps, blocks * LANES), 1), LANES), per)
        total = jnp.zeros((taps, blocks * LANES), f32)
        for g in range(tile_groups):
            total = jnp.where(group_of == g, dot(toep_a[q * tile_groups + g], window), total)
        for b in range(blocks):
            conv[b * taps : (b + 1) * taps, at] = total[:, b * LANES : (b + 1) * LANES]
        return carry

    lax.fori_loop(0, tiles, medium_tile, 0)
    product = proj[1] * conv[...]
    gated[...] = product.astype(bf16)
    gated_a_out[...] = product.T.astype(bf16)
    scatter_start(0, 1, oa)
    pump((2, 3), steps[1], steps[2])
    after = scatter_end(0, 1, hidden[...])
    abuf[mytp] = after
    gather_start(2, abuf)
    pump((2, 3), steps[2], steps[3])
    gather_wait(2, abuf)
    normalize(abuf, gain_b)
    pump((2, 3), steps[3], steps[4])
    own_copy(2).wait()
    own_copy(3).wait()
    ring_end(2)

    in_project(wb)

    def same_group(shape):
        return lax.div(iota(shape, 0), modes) == lax.div(iota(shape, 1), per)

    side = tile_groups * modes
    for q in range(tiles):
        at = slice(q * LANES, (q + 1) * LANES)
        ends = dot(to_end[q * side : (q + 1) * side, :], xin[:, at].astype(f32), highest)
        ends = jnp.where(same_group((side, LANES)), ends, 0.0)
        total = ends[0:modes]
        for g in range(1, tile_groups):
            total = total + ends[g * modes : (g + 1) * modes]
        states[me, :, at] = total

    def state_copy(off, slot, to):
        return pltpu.make_async_remote_copy(
            src_ref=states.at[slot],
            dst_ref=states.at[slot],
            send_sem=state_send.at[off - 1],
            recv_sem=state_recv.at[off - 1],
            device_id={"ctx": to},
            device_id_type=MESH,
        )

    def state_start(off, carry):
        state_copy(off, me, lax.rem(me + off, n)).start()
        return carry

    lax.fori_loop(1, n, state_start, 0)

    def long_tile(q, carry):
        at = lanes(q)
        values = xin[:, at]
        group_of = lax.div(iota((tokens, LANES), 1), per)
        total = jnp.zeros((tokens, LANES), f32)
        for g in range(tile_groups):
            total = jnp.where(group_of == g, dot(toep_b[q * tile_groups + g], values), total)
        conv[:, at] = total
        return carry

    lax.fori_loop(0, tiles, long_tile, 0)

    def state_wait(off, carry):
        state_copy(off, lax.rem(me - off + n, n), lax.rem(me + off, n)).wait_recv()
        return carry

    lax.fori_loop(1, n, state_wait, 0)

    def state_add(j, total):
        gap = jnp.maximum(me - 1 - j, 0).astype(f32) * tokens
        term = jnp.exp(-rate_mc[...] * gap) * states[j]
        return total + jnp.where(j < me, term, jnp.zeros_like(term))

    entering = lax.fori_loop(0, n, state_add, jnp.zeros((modes, channels), f32))
    for q in range(tiles):
        at = slice(q * LANES, (q + 1) * LANES)
        spread = jnp.concatenate([entering[:, at]] * tile_groups, axis=0)
        spread = jnp.where(same_group((side, LANES)), spread, 0.0)
        conv[:, at] += dot(from_start[:, q * side : (q + 1) * side], spread, highest)
    product = proj[1] * conv[...]
    gated[...] = product.astype(bf16)
    ring_end(3)
    scatter_start(1, 3, ob)
    gated_b_out[...] = product.T.astype(bf16)
    mixed[...] = scatter_end(1, 3, abuf[mytp])

    gather_sent(0, hbuf)
    gather_sent(2, abuf)
    scatter_sent(0, 1)
    scatter_sent(1, 3)

    def state_sent(off, carry):
        state_copy(off, me, lax.rem(me + off, n)).wait_send()
        return carry

    lax.fori_loop(1, n, state_sent, 0)

    def ring_sent(step, carry):
        for stream in range(4):
            for way in (0, 1):
                ring_copy(stream, way, step).wait_send()
        return carry

    lax.fori_loop(0, n - 1, ring_sent, 0)


def per_device(
    n,
    ntp,
    hidden,
    norm_gain_a,
    in_weight_a,
    mr_filter,
    out_weight_a,
    norm_gain_b,
    in_weight_b,
    li_rate,
    li_residue,
    out_weight_b,
):
    tokens, width = hidden.shape
    dn, channels = in_weight_a.shape[1:]
    on = out_weight_a.shape[1]
    features = width * ntp
    groups, taps = mr_filter.shape
    modes = li_rate.shape[1]
    mode_rows = jnp.stack([li_rate.reshape(-1), li_residue.reshape(-1)])
    rate_mc = jnp.repeat(li_rate.T, channels // groups, axis=1)
    vmem = pl.BlockSpec(memory_space=pltpu.VMEM)
    anywhere = pl.BlockSpec(memory_space=pl.ANY)
    flops = 2 * tokens * features * channels * 8 + 2 * tokens * channels * (tokens + 2 * taps) * 8
    return pl.pallas_call(
        functools.partial(kernel, n, ntp),
        out_shape=(
            jax.ShapeDtypeStruct((tokens, width), bf16),
            jax.ShapeDtypeStruct((channels, tokens), bf16),
            jax.ShapeDtypeStruct((channels, tokens), bf16),
        ),
        in_specs=[vmem, vmem, anywhere, vmem, anywhere, vmem, anywhere, vmem, vmem, vmem, vmem, anywhere],
        out_specs=(vmem, vmem, vmem),
        scratch_shapes=[
            pltpu.VMEM((3, features, channels), bf16),
            pltpu.VMEM((n, channels, on), bf16),
            pltpu.VMEM((3, features, channels), bf16),
            pltpu.VMEM((n, channels, on), bf16),
            pltpu.VMEM((ntp, tokens, width), bf16),
            pltpu.VMEM((ntp, tokens, width), bf16),
            pltpu.VMEM((tokens, features), bf16),
            pltpu.VMEM((3, tokens, channels), f32),
            pltpu.VMEM((tokens, channels), bf16),
            pltpu.VMEM((taps, channels), bf16),
            pltpu.VMEM((tokens, channels), f32),
            pltpu.VMEM((tokens, channels), bf16),
            pltpu.VMEM((2, ntp - 1, tokens, width), bf16),
            pltpu.VMEM((2, ntp - 1, tokens, width), bf16),
            pltpu.VMEM((n, modes, channels), f32),
            pltpu.VMEM((groups, taps, 2 * taps), bf16),
            pltpu.VMEM((groups, tokens, tokens), bf16),
            pltpu.VMEM((groups, taps), f32),
            pltpu.VMEM((groups, tokens), f32),
            pltpu.VMEM((groups * modes, tokens), f32),
            pltpu.VMEM((tokens, groups * modes), f32),
            pltpu.SemaphoreType.DMA((4, 2, n - 1)),
            pltpu.SemaphoreType.DMA((4, 2, n - 1)),
            pltpu.SemaphoreType.DMA((4, ntp - 1)),
            pltpu.SemaphoreType.DMA((4, ntp - 1)),
            pltpu.SemaphoreType.DMA((n - 1,)),
            pltpu.SemaphoreType.DMA((n - 1,)),
            pltpu.SemaphoreType.DMA((2,)),
            pltpu.SemaphoreType.DMA((4,)),
        ],
        cost_estimate=pl.CostEstimate(flops=flops, bytes_accessed=32 * 1024 * 1024, transcendentals=0),
        compiler_params=pltpu.CompilerParams(
            collective_id=0, has_side_effects=True, vmem_limit_bytes=56 * 1024 * 1024
        ),
    )(
        hidden,
        norm_gain_a.reshape(1, -1),
        in_weight_a,
        mr_filter,
        out_weight_a,
        norm_gain_b.reshape(1, -1),
        in_weight_b,
        li_rate,
        li_residue,
        mode_rows,
        rate_mc,
        out_weight_b,
    )


def solution(mesh):
    in_specs = (
        P("ctx", "tp"),
        P(),
        P(None, "ctx", "tp"),
        P("tp", None),
        P("tp", "ctx"),
        P(),
        P(None, "ctx", "tp"),
        P("tp", None),
        P("tp", None),
        P("tp", "ctx"),
    )
    out_specs = (P("ctx", "tp"), P("tp", "ctx"), P("tp", "ctx"))
    return jax.shard_map(
        functools.partial(per_device, mesh.shape["ctx"], mesh.shape["tp"]),
        mesh=mesh,
        in_specs=in_specs,
        out_specs=out_specs,
        check_vma=False,
    )
```

time: 426 us -> 195 us (0.46)
  waiting for transfers between devices: 334 us -> 0 us
  Pallas kernels: 0 us -> 187 us
  matrix products: 20 us -> 0 us
  blocking collectives: 18.6 us -> 0 us
  local copies, waits for them, and re-layouts: 20.7 us -> 5.99 us
  between operations: 14.6 us -> 0.67 us
  other arithmetic: 10.8 us -> 0.61 us
  starting transfers between devices: 7.02 us -> 0 us
    all_gather x6 -> x0, waiting for transfers between devices: 272 us -> none  [the longest x2 200 us: layer_inputs(): lax.all_gather(weight, 'ctx', axis=1, tiled=True)]
    pallas_call x0 -> x1, Pallas kernels: none -> 187 us  [per_device(): pl.pallas_call(functools.partial(kernel, n, ntp), out_shape=(jax.ShapeDty...]
    reduce_scatter x2 -> x0, waiting for transfers between devices: 47.4 us -> none  [the longest x1 24.2 us: per_device(): lax.psum_scatter(second_partial.astype(jnp.bfloat16), 'tp', scatter_dimen...]
    dot_general x9 -> x0, matrix products: 20 us -> none  [the longest x2 9.91 us: layer_inputs(): jnp.einsum('knc,tn->kct', lax.all_gather(weight, 'ctx', axis=1, tiled=Tru...]
    all_to_all x1 -> x0, blocking collectives: 18.6 us -> none  [per_device(): lax.all_to_all(long_whole.reshape(channel_count, full_length).astype(jnp....]
    all_to_all x1 -> x0, waiting for transfers between devices: 10.9 us -> none  [per_device(): lax.all_to_all(long_in, 'ctx', split_axis=0, concat_axis=1, tiled=True)]
    another operation x4 -> x2, local copies, waits for them, and re-layouts: 5.5 us -> 0.16 us  [per_device(): mode_rows = jnp.stack([li_rate.reshape(-1), li_residue.reshape(-1)])]
    slice x16 -> x0, local copies, waits for them, and re-layouts: 5.14 us -> none  [the longest x10 2.6 us: long_parts(): lax.associative_scan(chain_blocks, (block_end, block_decay), axis=2)]
  transfers between devices with their start and end apart: 10 -> 0, of which waited for: 9 -> 0; matrix products, arithmetic and copies ran while one was open for 9% -> 0% of each run, Pallas kernels for 0% -> 0%
where the time goes in v1:
time: 195 us; the launch traced here: 194 us
  Pallas kernels  187 us (96%)
  local copies, waits for them, and re-layouts  5.99 us (3%)
    pallas_call x1, Pallas kernels, per_device(): pl.pallas_call(functools.partial(kernel, n, ntp), out_shape=(jax.ShapeDty...  187 us
    unnamed x15, local copies, waits for them, and re-layouts  4.94 us

profile of v1, /device:TPU:0, one launch (start us, length us, event | category | flops | bytes accessed | tf_op | source)
XLA Modules:
  0.0 193.9 jit_solution(8437560594432521811)
XLA Ops:
  0.6 0.8 copy.20.residue
  1.4 0.0 copy-start.2
  1.4 0.0 copy-start.4
  1.4 0.1 stack_reshape.7
  1.5 0.6 copy-done.4
  2.1 0.1 copy.19.rate
  2.2 0.0 copy-done.2
  2.2 0.0 copy-start.3
  2.2 0.1 stack_reshape.6
  2.3 0.6 pad_maximum_fusion.mode_rows
  2.9 0.1 broadcast_in_dim.3
  3.0 0.0 copy-done.3
  3.0 0.8 reshape.17.rate_mc
  3.8 186.6 %shard_map.121 = (bf16[256,512]{1,0:T(8,128)(2,1)}, bf16[512,256]{1,0:T(8,128)(2,1)}, bf16[512,256]{1,0:T(8,128)(2,1)}) custom-call(bf16[256,512]{1,0:T(8,128)(2,1)} %hidden.1, f32[1,2048]{1,0:T(1,128)} %bitcast.4, bf16[3,256,512]{2,1,0:T(8,128)(2,1)} %win_a.1, bf16[32,128]{1,0:T(8,128)(2,1)} %mr_filter.1, bf16[512,256]{1,0:T(8,128)(2,1)} %wout_a.1, ...), custom_call_target="tpu_custom_call" | custom-call | flops 5368709120 | bytes 33554432 | tf_op jit(solution)/shard_map/pallas_call | solution.py:460
  190.4 0.0 copy-start.1
  190.4 1.7 copy.24
  192.1 0.0 copy-done.1
  192.1 0.0 copy-start
  192.1 0.7 copy.25
  192.8 0.3 copy-done
  193.2 0.7 copy.26
Async XLA Ops:
  1.4 0.8 copy-start.2
  1.4 0.7 copy-start.4
  2.2 0.8 copy-start.3
  190.4 1.7 copy-start.1
  192.1 1.0 copy-start

commit v2 on v1

v2 whole, which is shorter than its diff:
```python
import functools

import jax
import jax.numpy as jnp
from jax import lax
from jax.experimental import pallas as pl
from jax.experimental.pallas import tpu as pltpu
from jax.sharding import PartitionSpec as P

LANES = 128
MESH = pl.DeviceIdType.MESH
f32 = jnp.float32
bf16 = jnp.bfloat16
highest = lax.Precision.HIGHEST


def dot(a, b, precision=None):
    return lax.dot_general(
        a, b, (((1,), (0,)), ((), ())), precision=precision, preferred_element_type=f32
    )


def iota(shape, dim):
    return lax.broadcasted_iota(jnp.int32, shape, dim)


def kernel(
    n,
    ntp,
    hidden,
    gain_a,
    win_a,
    mr_filter,
    wout_a,
    gain_b,
    win_b,
    rate,
    residue,
    mode_rows,
    rate_mc,
    wout_b,
    mixed,
    gated_a_out,
    gated_b_out,
    wa,
    oa,
    wb,
    ob,
    hbuf,
    abuf,
    normed,
    proj,
    xin,
    halos,
    conv,
    gated,
    part,
    from_core,
    core_sum,
    from_first,
    first_sum,
    from_last,
    turned,
    turned_out,
    states,
    toep_a,
    toep_b,
    rows_a,
    rows_b,
    to_end,
    from_start,
    line_send,
    line_recv,
    cross_send,
    cross_recv,
    swap_send,
    swap_recv,
    state_send,
    state_recv,
    halo_send,
    halo_recv,
    local_sems,
):
    me = lax.axis_index("ctx")
    mytp = lax.axis_index("tp")
    tokens, width = hidden.shape
    all_channels = win_a.shape[2]
    channels = all_channels // 2
    dn = win_a.shape[1]
    on = wout_a.shape[1]
    features = width * ntp
    all_groups, taps = mr_filter.shape
    groups = all_groups // 2
    modes = rate.shape[1]
    per = channels // groups
    tile_groups = LANES // per
    tiles = channels // LANES
    blocks = tokens // taps
    depth = n // 2
    rows2 = tokens // 2

    z, y = lax.div(me, 2), lax.rem(me, 2)
    lo = lax.rem(z, 2)
    pair = lax.div(z, 2)
    x, core = lax.div(mytp, 2), lax.rem(mytp, 2)
    core_peer = {"tp": x * 2 + 1 - core}
    x_peer = {"tp": (1 - x) * 2 + core}
    z_peer = {"ctx": (z + 1 - 2 * lo) * 2 + y}
    y_peer = {"ctx": z * 2 + 1 - y}

    barrier = pltpu.get_barrier_semaphore()

    def greet_ctx(off, carry):
        pl.semaphore_signal(
            barrier, inc=1, device_id={"ctx": lax.rem(me + off, n)}, device_id_type=MESH
        )
        return carry

    lax.fori_loop(1, n, greet_ctx, 0)
    for peer in (core_peer, x_peer):
        pl.semaphore_signal(barrier, inc=1, device_id=peer, device_id_type=MESH)

    def remote(src, dst, send, recv, peer):
        return pltpu.make_async_remote_copy(
            src_ref=src,
            dst_ref=dst,
            send_sem=send,
            recv_sem=recv,
            device_id=peer,
            device_id_type=MESH,
        )

    streams = ((win_a, wa), (wout_a, oa), (win_b, wb), (wout_b, ob))

    def slot(stream, h, owner):
        buffer = streams[stream][1]
        if stream in (0, 2):
            return buffer.at[h, :, pl.ds(pl.multiple_of(owner * dn, dn), dn), :]
        return buffer.at[h, owner]

    def own(stream, h):
        source = streams[stream][0]
        at = pl.ds(pl.multiple_of(h * channels, channels), channels)
        return source.at[:, :, at] if stream in (0, 2) else source.at[at, :]

    def along(way):
        return (z, 1) if way == 0 else (depth - 1 - z, -1)

    def line_copy(stream, way, kind, step, first=False):
        zz, d = along(way)
        h = 1 - lo if kind == 0 else lo
        owner = (z - d * step) * 2 + y
        return remote(
            own(stream, h) if first else slot(stream, h, owner),
            slot(stream, h, owner),
            line_send.at[stream, way, kind, step],
            line_recv.at[stream, way, kind, step],
            {"ctx": (z + d) * 2 + y},
        )

    def line_arrival(stream, way, kind, step):
        zz, d = along(way)
        h = lo if kind == 0 else 1 - lo
        owner = (z - d * (step + 1)) * 2 + y
        here = slot(stream, h, owner)
        return remote(
            here,
            here,
            line_send.at[stream, way, kind, step],
            line_recv.at[stream, way, kind, step],
            {"ctx": (z - d) * 2 + y},
        )

    def cross_copy(stream, way, step, side):
        zz, d = along(way)
        owner = (z - d * step) * 2 + side
        here = slot(stream, lo, owner)
        return remote(
            here, here, cross_send.at[stream, way, step], cross_recv.at[stream, way, step], y_peer
        )

    def cross_own(stream):
        return remote(
            own(stream, lo),
            slot(stream, lo, me),
            cross_send.at[stream, 0, 0],
            cross_recv.at[stream, 0, 0],
            y_peer,
        )

    def start(stream):
        for way in (0, 1):
            zz, d = along(way)

            @pl.when(zz + 1 < depth)
            def near():
                line_copy(stream, way, 0, 0, True).start()

        for way in (0, 1):
            zz, d = along(way)

            @pl.when(zz + 2 < depth)
            def through():
                line_copy(stream, way, 1, 0, True).start()

        cross_own(stream).start()

    def pump_step(stream, step):
        for way in (0, 1):
            zz, d = along(way)

            @pl.when(zz - step >= 0)
            def arrived():
                line_arrival(stream, way, 0, step - 1).wait_recv()

                @pl.when(zz + 2 < depth)
                def through():
                    line_copy(stream, way, 1, step).start()

                cross_copy(stream, way, step, y).start()

                @pl.when(zz + 1 < depth)
                def near():
                    line_arrival(stream, way, 1, step - 1).wait_recv()
                    line_copy(stream, way, 0, step).start()

    def pump(stream, low, high):
        def body(step, carry):
            pump_step(stream, step)
            return carry

        if high > low:
            lax.fori_loop(low, high, body, 0)

    def finish(stream):
        cross_copy(stream, 0, 0, 1 - y).wait_recv()

        def body(step, carry):
            for way in (0, 1):
                zz, d = along(way)

                @pl.when(zz - step >= 0)
                def arrived():
                    cross_copy(stream, way, step, 1 - y).wait_recv()

            return carry

        lax.fori_loop(1, depth, body, 0)
        own_copy(stream).wait()

    def all_sent(stream):
        cross_own(stream).wait_send()

        def body(step, carry):
            for way in (0, 1):
                zz, d = along(way)

                @pl.when(zz - step >= 0)
                def passed():
                    @pl.when(zz + 1 < depth)
                    def near():
                        line_copy(stream, way, 0, step).wait_send()

                    @pl.when(zz + 2 < depth)
                    def through():
                        line_copy(stream, way, 1, step).wait_send()

                    @pl.when(step > 0)
                    def crossed():
                        cross_copy(stream, way, step, y).wait_send()

            return carry

        lax.fori_loop(0, depth, body, 0)

    def own_copy(stream):
        return pltpu.make_async_copy(own(stream, lo), slot(stream, lo, me), local_sems.at[stream])

    upper, lower = pl.ds(0, rows2), pl.ds(rows2, rows2)

    def swap(use, step, src, dst, peer):
        return remote(src, dst, swap_send.at[use, step], swap_recv.at[use, step], peer)

    def gather_moves(use, buffer):
        def move(step, ref_out, ref_in, peer):
            return (swap(use, step, ref_out, ref_out, peer), swap(use, step, ref_in, ref_in, peer))

        return (
            move(0, buffer.at[lo, x, core, upper], buffer.at[1 - lo, x, core, upper], z_peer),
            move(1, buffer.at[lo, x, core, lower], buffer.at[lo, 1 - x, core, lower], x_peer),
            move(2, buffer.at[:, x, core, upper], buffer.at[:, 1 - x, core, upper], x_peer),
            move(3, buffer.at[lo, :, core, lower], buffer.at[1 - lo, :, core, lower], z_peer),
            move(4, buffer.at[:, :, core], buffer.at[:, :, 1 - core], core_peer),
        )

    def gather_first(use, buffer):
        moves = gather_moves(use, buffer)
        moves[0][0].start()
        moves[1][0].start()

    def gather_second(use, buffer):
        moves = gather_moves(use, buffer)
        moves[0][1].wait_recv()
        moves[2][0].start()
        moves[1][1].wait_recv()
        moves[3][0].start()

    def gather_third(use, buffer):
        moves = gather_moves(use, buffer)
        moves[2][1].wait_recv()
        moves[3][1].wait_recv()
        moves[4][0].start()

    def gather_end(use, buffer):
        moves = gather_moves(use, buffer)
        moves[4][1].wait_recv()
        for out, into in moves:
            out.wait_send()

    def normalize(buffer, gain):
        for b in range(2):
            total = jnp.zeros((tokens, 1), f32)
            for block in range(ntp):
                wide = buffer[b, block // 2, block % 2].astype(f32)
                total = total + jnp.sum(wide * wide, axis=1, keepdims=True)
            factor = lax.rsqrt(total / features + 1e-06)
            for block in range(ntp):
                at = slice(block * width, (block + 1) * width)
                wide = buffer[b, block // 2, block % 2].astype(f32)
                normed[b * tokens : (b + 1) * tokens, at] = (wide * factor * gain[:, at]).astype(bf16)

    def in_project(weight):
        def body(k, carry):
            proj[k] = dot(normed[...], weight[lo, k])
            return carry

        lax.fori_loop(0, 3, body, 0)
        xin[...] = (proj[0] * proj[2]).astype(bf16)

    def out_blocks(buffer, c):
        def body(xx, carry):
            for j in range(width // on):
                block = dot(gated[...], buffer[lo, (xx * 2 + c) * (width // on) + j]).astype(bf16)
                for b in range(2):
                    part[b, xx, c, :, j * on : (j + 1) * on] = block[b * tokens : (b + 1) * tokens]
            return carry

        lax.fori_loop(0, 2, body, 0)

    def scatter_moves(which):
        use = 2 + which
        return (
            swap(use, 0, part.at[:, :, 1 - core], from_core.at[which], core_peer),
            swap(use, 1, core_sum.at[1 - lo, :, upper], from_first.at[which, 0], z_peer),
            swap(use, 2, core_sum.at[:, 1 - x, lower], from_first.at[which, 1], x_peer),
            swap(use, 3, first_sum.at[0, 1 - x], from_last.at[which, 0], x_peer),
            swap(use, 4, first_sum.at[1, 1 - lo], from_last.at[which, 1], z_peer),
        )

    def scatter_first(which, buffer):
        moves = scatter_moves(which)
        out_blocks(buffer, 1 - core)
        moves[0].start()
        out_blocks(buffer, core)

    def scatter_second(which):
        moves = scatter_moves(which)
        moves[0].wait_recv()

        def add(b, xx, at):
            core_sum[b, xx, at] = (
                part[b, xx, core, at].astype(f32) + from_core[which, b, xx, at].astype(f32)
            ).astype(bf16)

        for xx in range(2):
            add(1 - lo, xx, upper)
        moves[1].start()
        for b in range(2):
            add(b, 1 - x, lower)
        moves[2].start()
        for xx in range(2):
            add(lo, xx, upper)
        for b in range(2):
            add(b, x, lower)

    def scatter_third(which):
        moves = scatter_moves(which)
        moves[1].wait_recv()
        for xx in range(2):
            first_sum[0, xx] = (
                core_sum[lo, xx, upper].astype(f32) + from_first[which, 0, xx].astype(f32)
            ).astype(bf16)
        moves[3].start()
        moves[2].wait_recv()
        for b in range(2):
            first_sum[1, b] = (
                core_sum[b, x, lower].astype(f32) + from_first[which, 1, b].astype(f32)
            ).astype(bf16)
        moves[4].start()

    def scatter_end(which, base, out):
        moves = scatter_moves(which)
        moves[3].wait_recv()
        out[upper] = (
            base[upper].astype(f32) + first_sum[0, x].astype(f32) + from_last[which, 0].astype(f32)
        ).astype(bf16)
        moves[4].wait_recv()
        out[lower] = (
            base[lower].astype(f32) + first_sum[1, lo].astype(f32) + from_last[which, 1].astype(f32)
        ).astype(bf16)
        for move in moves:
            move.wait_send()

    def give_move(which):
        return swap(
            4, which, turned.at[which], turned_out.at[which, pl.ds(pl.multiple_of(lo * channels, channels), channels)], z_peer
        )

    def give_back(which, product):
        flat = product.T.astype(bf16)
        at = pl.ds(pl.multiple_of(lo * channels, channels), channels)
        own_block = jnp.where(lo == 0, flat[:, :tokens], flat[:, tokens:])
        other = jnp.where(lo == 0, flat[:, tokens:], flat[:, :tokens])
        turned[which] = other
        turned_out[which, at] = own_block
        give_move(which).start()

    def give_end(which):
        give_move(which).wait_send()
        arriving = turned_out.at[which, pl.ds(pl.multiple_of((1 - lo) * channels, channels), channels)]
        swap(4, which, turned.at[which], arriving, z_peer).wait_recv()

    def lanes(q):
        return pl.ds(pl.multiple_of(q * LANES, LANES), LANES)

    hbuf[lo, x, core] = hidden[...]
    for stream in range(4):
        own_copy(stream).start()
    pl.semaphore_wait(barrier, (n - 1) + 2)

    gather_first(0, hbuf)
    start(0)
    start(1)

    flip = (lax.rem(iota((taps, taps), 0) + iota((taps, taps), 1), taps) == 0).astype(bf16)
    rows_a[...] = dot(mr_filter[...], flip)
    lag = lax.rem(tokens - iota((all_groups, tokens), 1), tokens).astype(f32)
    impulse = jnp.zeros((all_groups, tokens), f32)
    for m in range(modes):
        r = rate[:, m : m + 1]
        impulse = impulse + residue[:, m : m + 1] * jnp.sqrt(2.0 * r) * jnp.exp(-r * lag)
    rows_b[...] = impulse

    def build_a(g, carry):
        row = jnp.broadcast_to(rows_a[pl.ds(lo * groups + g, 1), :], (taps, taps))
        rolled = pltpu.roll(row, 0, 1, stride=1, stride_axis=0)
        below = iota((taps, taps), 1) <= iota((taps, taps), 0)
        toep_a[g, :, :taps] = jnp.where(below, 0.0, rolled).astype(bf16)
        toep_a[g, :, taps:] = jnp.where(below, rolled, 0.0).astype(bf16)
        return carry

    def build_b(g, carry):
        row = jnp.broadcast_to(rows_b[pl.ds(lo * groups + g, 1), :], (tokens, tokens))
        rolled = pltpu.roll(row, 0, 1, stride=1, stride_axis=0)
        below = iota((tokens, tokens), 1) <= iota((tokens, tokens), 0)
        toep_b[g] = jnp.where(below, rolled, 0.0).astype(bf16)
        return carry

    lax.fori_loop(0, groups, build_a, 0)
    gather_second(0, hbuf)
    lax.fori_loop(0, groups, build_b, 0)
    gather_third(0, hbuf)

    mode_lanes = pl.ds(pl.multiple_of(lo * groups * modes, LANES), groups * modes)
    rate_row = mode_rows[0:1, mode_lanes]
    weight_row = mode_rows[1:2, mode_lanes] * jnp.sqrt(2.0 * rate_row)
    position = iota((tokens, groups * modes), 0).astype(f32)
    from_start[...] = weight_row * jnp.exp(-rate_row * (position + 1.0))
    to_end[...] = jnp.exp(-rate_row * (tokens - 1.0 - position)).T

    pump(0, 1, 2)
    pump(1, 1, 2)
    gather_end(0, hbuf)
    normalize(hbuf, gain_a)
    for step in range(2, 4):
        pump(0, step, step + 1)
        pump(1, step, step + 1)
    pump(0, 4, depth)
    pump(1, 4, depth)
    start(2)
    finish(0)

    in_project(wa)

    def tail(b):
        return xin.at[pl.ds((b + 1) * tokens - taps, taps), :]

    halo_moves = (
        remote(tail(0), halos.at[0], halo_send.at[0], halo_recv.at[0], y_peer),
        remote(tail(1), halos.at[1], halo_send.at[1], halo_recv.at[1], y_peer),
        remote(
            tail(1),
            halos.at[2],
            halo_send.at[2],
            halo_recv.at[2],
            {"ctx": lax.rem(z + 2, depth) * 2 + 1 - y},
        ),
    )
    for move in halo_moves:
        move.start()
    pump(2, 1, 2)
    start(3)
    for move in halo_moves:
        move.wait()

    def medium_tile(q, carry):
        at = lanes(q)
        near0, near1, far = halos[0, :, at], halos[1, :, at], halos[2, :, at]
        far = jnp.where(z >= 2, far, jnp.zeros_like(far))
        befores = (jnp.where(y == 1, near0, far), jnp.where(y == 1, near1, near0))
        here, early = [], []
        for b in range(2):
            mine = [
                xin[b * tokens + k * taps : b * tokens + (k + 1) * taps, at] for k in range(blocks)
            ]
            here = here + mine
            early = early + [befores[b]] + mine[:-1]
        window = jnp.concatenate(
            [jnp.concatenate(early, axis=1), jnp.concatenate(here, axis=1)], axis=0
        )
        shape = (taps, 2 * blocks * LANES)
        group_of = lax.div(lax.rem(iota(shape, 1), LANES), per)
        total = jnp.zeros(shape, f32)
        for g in range(tile_groups):
            total = jnp.where(group_of == g, dot(toep_a[q * tile_groups + g], window), total)
        for k in range(2 * blocks):
            conv[k * taps : (k + 1) * taps, at] = total[:, k * LANES : (k + 1) * LANES]
        return carry

    lax.fori_loop(0, tiles, medium_tile, 0)
    product = proj[1] * conv[...]
    gated[...] = product.astype(bf16)
    finish(1)
    scatter_first(0, oa)
    give_back(0, product)
    scatter_second(0)
    pump(2, 2, 3)
    scatter_third(0)
    pump(3, 1, 2)
    scatter_end(0, hidden, abuf.at[lo, x, core])
    gather_first(1, abuf)
    pump(2, 3, depth)
    gather_second(1, abuf)
    pump(3, 2, 3)
    gather_third(1, abuf)
    gather_end(1, abuf)
    normalize(abuf, gain_b)
    finish(2)

    in_project(wb)

    def same_group(shape):
        return lax.div(iota(shape, 0), modes) == lax.div(iota(shape, 1), per)

    side = tile_groups * modes
    mine = pair * 2 + y
    for b in range(2):
        for q in range(tiles):
            at = slice(q * LANES, (q + 1) * LANES)
            values = xin[b * tokens : (b + 1) * tokens, at].astype(f32)
            ends = dot(to_end[q * side : (q + 1) * side, :], values, highest)
            ends = jnp.where(same_group((side, LANES)), ends, 0.0)
            total = ends[0:modes]
            for g in range(1, tile_groups):
                total = total + ends[g * modes : (g + 1) * modes]
            states[mine, b, :, at] = total

    def state_copy(off, index, to):
        return remote(
            states.at[index],
            states.at[index],
            state_send.at[off - 1],
            state_recv.at[off - 1],
            {"ctx": (lax.div(to, 2) * 2 + lo) * 2 + lax.rem(to, 2)},
        )

    def state_start(off, carry):
        state_copy(off, mine, lax.rem(mine + off, depth)).start()
        return carry

    lax.fori_loop(1, depth, state_start, 0)
    pump(3, 3, depth)

    def long_tile(q, carry):
        at = lanes(q)
        values = jnp.concatenate([xin[0:tokens, at], xin[tokens : 2 * tokens, at]], axis=1)
        group_of = lax.div(lax.rem(iota((tokens, 2 * LANES), 1), LANES), per)
        total = jnp.zeros((tokens, 2 * LANES), f32)
        for g in range(tile_groups):
            total = jnp.where(group_of == g, dot(toep_b[q * tile_groups + g], values), total)
        for b in range(2):
            conv[b * tokens : (b + 1) * tokens, at] = total[:, b * LANES : (b + 1) * LANES]
        return carry

    lax.fori_loop(0, tiles, long_tile, 0)

    def state_wait(off, carry):
        state_copy(off, lax.rem(mine - off + depth, depth), lax.rem(mine + off, depth)).wait_recv()
        return carry

    lax.fori_loop(1, depth, state_wait, 0)
    rates = rate_mc[:, pl.ds(pl.multiple_of(lo * channels, channels), channels)]

    def state_add(index, totals):
        result = []
        for b in range(2):
            block = 4 * pair + 2 * b + y
            total = totals[b]
            for k in range(2):
                j = 4 * lax.div(index, 2) + 2 * k + lax.rem(index, 2)
                gap = jnp.maximum(block - 1 - j, 0).astype(f32) * tokens
                term = jnp.exp(-rates * gap) * states[index, k]
                total = total + jnp.where(j < block, term, jnp.zeros_like(term))
            result.append(total)
        return tuple(result)

    zero = jnp.zeros((modes, channels), f32)
    entering = lax.fori_loop(0, depth, state_add, (zero, zero))
    for b in range(2):
        for q in range(tiles):
            at = slice(q * LANES, (q + 1) * LANES)
            spread = jnp.concatenate([entering[b][:, at]] * tile_groups, axis=0)
            spread = jnp.where(same_group((side, LANES)), spread, 0.0)
            conv[b * tokens : (b + 1) * tokens, at] += dot(
                from_start[:, q * side : (q + 1) * side], spread, highest
            )
    product = proj[1] * conv[...]
    gated[...] = product.astype(bf16)
    finish(3)
    scatter_first(1, ob)
    give_back(1, product)
    scatter_second(1)
    scatter_third(1)
    scatter_end(1, abuf.at[lo, x, core], mixed)

    give_end(0)
    give_end(1)
    gated_a_out[...] = turned_out[0]
    gated_b_out[...] = turned_out[1]

    def state_sent(off, carry):
        state_copy(off, mine, lax.rem(mine + off, depth)).wait_send()
        return carry

    lax.fori_loop(1, depth, state_sent, 0)
    for stream in range(4):
        all_sent(stream)


def per_device(
    n,
    ntp,
    hidden,
    norm_gain_a,
    in_weight_a,
    mr_filter,
    out_weight_a,
    norm_gain_b,
    in_weight_b,
    li_rate,
    li_residue,
    out_weight_b,
):
    tokens, width = hidden.shape
    dn, channels = in_weight_a.shape[1:]
    on = out_weight_a.shape[1]
    features = width * ntp
    groups, taps = mr_filter.shape
    modes = li_rate.shape[1]
    half = channels // 2
    mode_rows = jnp.stack([li_rate.reshape(-1), li_residue.reshape(-1)])
    rate_mc = jnp.repeat(li_rate.T, channels // groups, axis=1)
    vmem = pl.BlockSpec(memory_space=pltpu.VMEM)
    anywhere = pl.BlockSpec(memory_space=pl.ANY)
    flops = 2 * tokens * features * channels * 8 + 2 * tokens * channels * (tokens + 2 * taps) * 8
    return pl.pallas_call(
        functools.partial(kernel, n, ntp),
        out_shape=(
            jax.ShapeDtypeStruct((tokens, width), bf16),
            jax.ShapeDtypeStruct((channels, tokens), bf16),
            jax.ShapeDtypeStruct((channels, tokens), bf16),
        ),
        in_specs=[vmem, vmem, anywhere, vmem, anywhere, vmem, anywhere, vmem, vmem, vmem, vmem, anywhere],
        out_specs=(vmem, vmem, vmem),
        scratch_shapes=[
            pltpu.VMEM((2, 3, features, half), bf16),
            pltpu.VMEM((2, n, half, on), bf16),
            pltpu.VMEM((2, 3, features, half), bf16),
            pltpu.VMEM((2, n, half, on), bf16),
            pltpu.VMEM((2, 2, 2, tokens, width), bf16),
            pltpu.VMEM((2, 2, 2, tokens, width), bf16),
            pltpu.VMEM((2 * tokens, features), bf16),
            pltpu.VMEM((3, 2 * tokens, half), f32),
            pltpu.VMEM((2 * tokens, half), bf16),
            pltpu.VMEM((3, taps, half), bf16),
            pltpu.VMEM((2 * tokens, half), f32),
            pltpu.VMEM((2 * tokens, half), bf16),
            pltpu.VMEM((2, 2, 2, tokens, width), bf16),
            pltpu.VMEM((2, 2, 2, tokens, width), bf16),
            pltpu.VMEM((2, 2, tokens, width), bf16),
            pltpu.VMEM((2, 2, 2, tokens // 2, width), bf16),
            pltpu.VMEM((2, 2, tokens // 2, width), bf16),
            pltpu.VMEM((2, 2, tokens // 2, width), bf16),
            pltpu.VMEM((2, half, tokens), bf16),
            pltpu.VMEM((2, channels, tokens), bf16),
            pltpu.VMEM((n // 2, 2, modes, half), f32),
            pltpu.VMEM((groups // 2, taps, 2 * taps), bf16),
            pltpu.VMEM((groups // 2, tokens, tokens), bf16),
            pltpu.VMEM((groups, taps), f32),
            pltpu.VMEM((groups, tokens), f32),
            pltpu.VMEM((groups // 2 * modes, tokens), f32),
            pltpu.VMEM((tokens, groups // 2 * modes), f32),
            pltpu.SemaphoreType.DMA((4, 2, 2, n // 2)),
            pltpu.SemaphoreType.DMA((4, 2, 2, n // 2)),
            pltpu.SemaphoreType.DMA((4, 2, n // 2)),
            pltpu.SemaphoreType.DMA((4, 2, n // 2)),
            pltpu.SemaphoreType.DMA((5, 5)),
            pltpu.SemaphoreType.DMA((5, 5)),
            pltpu.SemaphoreType.DMA((n // 2 - 1,)),
            pltpu.SemaphoreType.DMA((n // 2 - 1,)),
            pltpu.SemaphoreType.DMA((3,)),
            pltpu.SemaphoreType.DMA((3,)),
            pltpu.SemaphoreType.DMA((4,)),
        ],
        cost_estimate=pl.CostEstimate(flops=flops, bytes_accessed=32 * 1024 * 1024, transcendentals=0),
        compiler_params=pltpu.CompilerParams(
            collective_id=0, has_side_effects=True, vmem_limit_bytes=60 * 1024 * 1024
        ),
    )(
        hidden,
        norm_gain_a.reshape(1, -1),
        in_weight_a,
        mr_filter,
        out_weight_a,
        norm_gain_b.reshape(1, -1),
        in_weight_b,
        li_rate,
        li_residue,
        mode_rows,
        rate_mc,
        out_weight_b,
    )


def solution(mesh):
    in_specs = (
        P("ctx", "tp"),
        P(),
        P(None, "ctx", "tp"),
        P("tp", None),
        P("tp", "ctx"),
        P(),
        P(None, "ctx", "tp"),
        P("tp", None),
        P("tp", None),
        P("tp", "ctx"),
    )
    out_specs = (P("ctx", "tp"), P("tp", "ctx"), P("tp", "ctx"))
    return jax.shard_map(
        functools.partial(per_device, mesh.shape["ctx"], mesh.shape["tp"]),
        mesh=mesh,
        in_specs=in_specs,
        out_specs=out_specs,
        check_vma=False,
    )
```

time: 195 us -> 168 us (0.86)
  Pallas kernels: 187 us -> 160 us
    pallas_call x1, Pallas kernels: 187 us -> 160 us  [per_device(): pl.pallas_call(functools.partial(kernel, n, ntp), out_shape=(jax.ShapeDty...]
where the time goes in v2:
time: 168 us; the launch traced here: 167 us
  Pallas kernels  160 us (95%)
  local copies, waits for them, and re-layouts  5.99 us (4%)
    pallas_call x1, Pallas kernels, per_device(): pl.pallas_call(functools.partial(kernel, n, ntp), out_shape=(jax.ShapeDty...  160 us
    unnamed x15, local copies, waits for them, and re-layouts  4.94 us

profile of v2, /device:TPU:0, one launch (start us, length us, event | category | flops | bytes accessed | tf_op | source)
XLA Modules:
  0.0 167.3 jit_solution(16898186472384329241)
XLA Ops:
  0.6 0.8 copy.20.residue
  1.4 0.0 copy-start.2
  1.4 0.0 copy-start.4
  1.4 0.1 stack_reshape.7
  1.5 0.6 copy-done.4
  2.1 0.1 copy.19.rate
  2.2 0.0 copy-done.2
  2.2 0.0 copy-start.3
  2.2 0.1 stack_reshape.6
  2.3 0.6 pad_maximum_fusion.mode_rows
  2.9 0.1 broadcast_in_dim.3
  3.0 0.0 copy-done.3
  3.0 0.8 reshape.17.rate_mc
  3.8 160.1 %shard_map.121 = (bf16[256,512]{1,0:T(8,128)(2,1)}, bf16[512,256]{1,0:T(8,128)(2,1)}, bf16[512,256]{1,0:T(8,128)(2,1)}) custom-call(bf16[256,512]{1,0:T(8,128)(2,1)} %hidden.1, f32[1,2048]{1,0:T(1,128)} %bitcast.4, bf16[3,256,512]{2,1,0:T(8,128)(2,1)} %win_a.1, bf16[32,128]{1,0:T(8,128)(2,1)} %mr_filter.1, bf16[512,256]{1,0:T(8,128)(2,1)} %wout_a.1, ...), custom_call_target="tpu_custom_call" | custom-call | flops 5368709120 | bytes 33554432 | tf_op jit(solution)/shard_map/pallas_call | solution.py:686
  163.9 0.0 copy-start.1
  163.9 1.7 %copy.24 = bf16[256,512]{1,0:T(8,128)(2,1)} copy(bf16[256,512]{1,0:T(8,128)(2,1)} %get-tuple-element.6) | data formatting | bytes 524288
  165.6 0.0 copy-done.1
  165.6 0.0 copy-start
  165.6 0.7 copy.25
  166.3 0.3 copy-done
  166.6 0.7 copy.26
Async XLA Ops:
  1.4 0.8 copy-start.2
  1.4 0.7 copy-start.4
  2.2 0.8 copy-start.3
  163.9 1.7 %copy-start.1 = (bf16[512,256]{1,0:T(8,128)(2,1)S(1)}, bf16[512,256]{1,0:T(8,128)(2,1)}, u32[]{:S(2)}) copy-start(bf16[512,256]{1,0:T(8,128)(2,1)} %get-tuple-element.7) | copy-start | bytes 786436
  165.6 1.0 copy-start

commit v3 on v2

--- a/solution.py
+++ b/solution.py
@@ -36,8 +36,6 @@
     win_b,
     rate,
     residue,
-    mode_rows,
-    rate_mc,
     wout_b,
     mixed,
     gated_a_out,
@@ -69,6 +67,7 @@
     rows_b,
     to_end,
     from_start,
+    rates_here,
     line_send,
     line_recv,
     cross_send,
@@ -132,11 +131,11 @@
 
     streams = ((win_a, wa), (wout_a, oa), (win_b, wb), (wout_b, ob))
 
-    def slot(stream, h, owner):
+    def slot(stream, owner):
         buffer = streams[stream][1]
         if stream in (0, 2):
-            return buffer.at[h, :, pl.ds(pl.multiple_of(owner * dn, dn), dn), :]
-        return buffer.at[h, owner]
+            return buffer.at[:, pl.ds(pl.multiple_of(owner * dn, dn), dn), :]
+        return buffer.at[owner]
 
     def own(stream, h):
         source = streams[stream][0]
@@ -146,35 +145,30 @@
     def along(way):
         return (z, 1) if way == 0 else (depth - 1 - z, -1)
 
-    def line_copy(stream, way, kind, step, first=False):
+    def line_copy(stream, way, step):
         zz, d = along(way)
-        h = 1 - lo if kind == 0 else lo
-        owner = (z - d * step) * 2 + y
         return remote(
-            own(stream, h) if first else slot(stream, h, owner),
-            slot(stream, h, owner),
-            line_send.at[stream, way, kind, step],
-            line_recv.at[stream, way, kind, step],
-            {"ctx": (z + d) * 2 + y},
-        )
-
-    def line_arrival(stream, way, kind, step):
+            own(stream, lax.rem(z + step, 2)),
+            slot(stream, me),
+            line_send.at[stream, way, step],
+            line_recv.at[stream, way, step],
+            {"ctx": (z + d * step) * 2 + y},
+        )
+
+    def line_arrival(stream, way, step):
         zz, d = along(way)
-        h = lo if kind == 0 else 1 - lo
-        owner = (z - d * (step + 1)) * 2 + y
-        here = slot(stream, h, owner)
+        here = slot(stream, (z - d * step) * 2 + y)
         return remote(
             here,
             here,
-            line_send.at[stream, way, kind, step],
-            line_recv.at[stream, way, kind, step],
-            {"ctx": (z - d) * 2 + y},
+            line_send.at[stream, way, step],
+            line_recv.at[stream, way, step],
+            {"ctx": (z - d * step) * 2 + y},
         )
 
     def cross_copy(stream, way, step, side):
         zz, d = along(way)
-        owner = (z - d * step) * 2 + side
-        here = slot(stream, lo, owner)
+        here = slot(stream, (z - d * step) * 2 + side)
         return remote(
             here, here, cross_send.at[stream, way, step], cross_recv.at[stream, way, step], y_peer
         )
@@ -182,63 +176,49 @@
     def cross_own(stream):
         return remote(
             own(stream, lo),
-            slot(stream, lo, me),
+            slot(stream, me),
             cross_send.at[stream, 0, 0],
             cross_recv.at[stream, 0, 0],
             y_peer,
         )
 
     def start(stream):
-        for way in (0, 1):
-            zz, d = along(way)
-
-            @pl.when(zz + 1 < depth)
-            def near():
-                line_copy(stream, way, 0, 0, True).start()
-
-        for way in (0, 1):
-            zz, d = along(way)
-
-            @pl.when(zz + 2 < depth)
-            def through():
-                line_copy(stream, way, 1, 0, True).start()
-
         cross_own(stream).start()
-
-    def pump_step(stream, step):
-        for way in (0, 1):
-            zz, d = along(way)
-
-            @pl.when(zz - step >= 0)
-            def arrived():
-                line_arrival(stream, way, 0, step - 1).wait_recv()
-
-                @pl.when(zz + 2 < depth)
-                def through():
-                    line_copy(stream, way, 1, step).start()
-
-                cross_copy(stream, way, step, y).start()
-
-                @pl.when(zz + 1 < depth)
-                def near():
-                    line_arrival(stream, way, 1, step - 1).wait_recv()
-                    line_copy(stream, way, 0, step).start()
-
-    def pump(stream, low, high):
-        def body(step, carry):
-            pump_step(stream, step)
-            return carry
-
-        if high > low:
-            lax.fori_loop(low, high, body, 0)
-
-    def finish(stream):
-        cross_copy(stream, 0, 0, 1 - y).wait_recv()
 
         def body(step, carry):
             for way in (0, 1):
                 zz, d = along(way)
 
+                @pl.when(zz + step < depth)
+                def ahead():
+                    line_copy(stream, way, step).start()
+
+            return carry
+
+        lax.fori_loop(1, depth, body, 0)
+
+    def pump(stream, low, high):
+        def body(step, carry):
+            for way in (0, 1):
+                zz, d = along(way)
+
+                @pl.when(zz - step >= 0)
+                def arrived():
+                    line_arrival(stream, way, step).wait_recv()
+                    cross_copy(stream, way, step, y).start()
+
+            return carry
+
+        if high > low:
+            lax.fori_loop(low, high, body, 0)
+
+    def finish(stream):
+        cross_copy(stream, 0, 0, 1 - y).wait_recv()
+
+        def body(step, carry):
+            for way in (0, 1):
+                zz, d = along(way)
+
                 @pl.when(zz - step >= 0)
                 def arrived():
                     cross_copy(stream, way, step, 1 - y).wait_recv()
@@ -255,26 +235,20 @@
             for way in (0, 1):
                 zz, d = along(way)
 
+                @pl.when(zz + step < depth)
+                def ahead():
+                    line_copy(stream, way, step).wait_send()
+
                 @pl.when(zz - step >= 0)
-                def passed():
-                    @pl.when(zz + 1 < depth)
-                    def near():
-                        line_copy(stream, way, 0, step).wait_send()
-
-                    @pl.when(zz + 2 < depth)
-                    def through():
-                        line_copy(stream, way, 1, step).wait_send()
-
-                    @pl.when(step > 0)
-                    def crossed():
-                        cross_copy(stream, way, step, y).wait_send()
+                def crossed():
+                    cross_copy(stream, way, step, y).wait_send()
 
             return carry
 
-        lax.fori_loop(0, depth, body, 0)
+        lax.fori_loop(1, depth, body, 0)
 
     def own_copy(stream):
-        return pltpu.make_async_copy(own(stream, lo), slot(stream, lo, me), local_sems.at[stream])
+        return pltpu.make_async_copy(own(stream, lo), slot(stream, me), local_sems.at[stream])
 
     upper, lower = pl.ds(0, rows2), pl.ds(rows2, rows2)
 
@@ -331,7 +305,7 @@
 
     def in_project(weight):
         def body(k, carry):
-            proj[k] = dot(normed[...], weight[lo, k])
+            proj[k] = dot(normed[...], weight[k])
             return carry
 
         lax.fori_loop(0, 3, body, 0)
@@ -340,7 +314,7 @@
     def out_blocks(buffer, c):
         def body(xx, carry):
             for j in range(width // on):
-                block = dot(gated[...], buffer[lo, (xx * 2 + c) * (width // on) + j]).astype(bf16)
+                block = dot(gated[...], buffer[(xx * 2 + c) * (width // on) + j]).astype(bf16)
                 for b in range(2):
                     part[b, xx, c, :, j * on : (j + 1) * on] = block[b * tokens : (b + 1) * tokens]
             return carry
@@ -471,9 +445,21 @@
     lax.fori_loop(0, groups, build_b, 0)
     gather_third(0, hbuf)
 
-    mode_lanes = pl.ds(pl.multiple_of(lo * groups * modes, LANES), groups * modes)
-    rate_row = mode_rows[0:1, mode_lanes]
-    weight_row = mode_rows[1:2, mode_lanes] * jnp.sqrt(2.0 * rate_row)
+    def mode_row(ref):
+        here = ref[pl.ds(pl.multiple_of(lo * groups, 8), groups), :]
+        shape = (modes, groups * modes)
+        pick = (iota(shape, 0) == lax.rem(iota(shape, 1), modes)).astype(f32)
+        spread = dot(here, pick, highest)
+        keep = iota(spread.shape, 0) == lax.div(iota(spread.shape, 1), modes)
+        return jnp.sum(jnp.where(keep, spread, 0.0), axis=0, keepdims=True)
+
+    rate_row = mode_row(rate)
+    weight_row = mode_row(residue) * jnp.sqrt(2.0 * rate_row)
+    shape = (modes, groups * modes)
+    by_mode = jnp.where(iota(shape, 0) == lax.rem(iota(shape, 1), modes), rate_row, 0.0)
+    shape = (groups * modes, channels)
+    pick = (lax.div(iota(shape, 0), modes) == lax.div(iota(shape, 1), per)).astype(f32)
+    rates_here[...] = dot(by_mode, pick, highest)
     position = iota((tokens, groups * modes), 0).astype(f32)
     from_start[...] = weight_row * jnp.exp(-rate_row * (position + 1.0))
     to_end[...] = jnp.exp(-rate_row * (tokens - 1.0 - position)).T
@@ -482,12 +468,11 @@
     pump(1, 1, 2)
     gather_end(0, hbuf)
     normalize(hbuf, gain_a)
-    for step in range(2, 4):
-        pump(0, step, step + 1)
-        pump(1, step, step + 1)
-    pump(0, 4, depth)
-    pump(1, 4, depth)
+    pump(0, 2, 3)
+    pump(1, 2, 3)
+    pump(0, 3, depth)
     start(2)
+    pump(1, 3, depth)
     finish(0)
 
     in_project(wa)
@@ -508,8 +493,6 @@
     )
     for move in halo_moves:
         move.start()
-    pump(2, 1, 2)
-    start(3)
     for move in halo_moves:
         move.wait()
 
@@ -543,20 +526,22 @@
     finish(1)
     scatter_first(0, oa)
     give_back(0, product)
+    pump(2, 1, 2)
+    start(3)
     scatter_second(0)
+    scatter_third(0)
     pump(2, 2, 3)
-    scatter_third(0)
-    pump(3, 1, 2)
     scatter_end(0, hidden, abuf.at[lo, x, core])
     gather_first(1, abuf)
+    gather_second(1, abuf)
     pump(2, 3, depth)
-    gather_second(1, abuf)
-    pump(3, 2, 3)
     gather_third(1, abuf)
+    pump(3, 1, 2)
     gather_end(1, abuf)
     normalize(abuf, gain_b)
     finish(2)
 
+    pump(3, 2, 3)
     in_project(wb)
 
     def same_group(shape):
@@ -609,7 +594,7 @@
         return carry
 
     lax.fori_loop(1, depth, state_wait, 0)
-    rates = rate_mc[:, pl.ds(pl.multiple_of(lo * channels, channels), channels)]
+    rates = rates_here[...]
 
     def state_add(index, totals):
         result = []
@@ -678,8 +663,6 @@
     groups, taps = mr_filter.shape
     modes = li_rate.shape[1]
     half = channels // 2
-    mode_rows = jnp.stack([li_rate.reshape(-1), li_residue.reshape(-1)])
-    rate_mc = jnp.repeat(li_rate.T, channels // groups, axis=1)
     vmem = pl.BlockSpec(memory_space=pltpu.VMEM)
     anywhere = pl.BlockSpec(memory_space=pl.ANY)
     flops = 2 * tokens * features * channels * 8 + 2 * tokens * channels * (tokens + 2 * taps) * 8
@@ -690,13 +673,13 @@
             jax.ShapeDtypeStruct((channels, tokens), bf16),
             jax.ShapeDtypeStruct((channels, tokens), bf16),
         ),
-        in_specs=[vmem, vmem, anywhere, vmem, anywhere, vmem, anywhere, vmem, vmem, vmem, vmem, anywhere],
+        in_specs=[vmem, vmem, anywhere, vmem, anywhere, vmem, anywhere, vmem, vmem, anywhere],
         out_specs=(vmem, vmem, vmem),
         scratch_shapes=[
-            pltpu.VMEM((2, 3, features, half), bf16),
-            pltpu.VMEM((2, n, half, on), bf16),
-            pltpu.VMEM((2, 3, features, half), bf16),
-            pltpu.VMEM((2, n, half, on), bf16),
+            pltpu.VMEM((3, features, half), bf16),
+            pltpu.VMEM((n, half, on), bf16),
+            pltpu.VMEM((3, features, half), bf16),
+            pltpu.VMEM((n, half, on), bf16),
             pltpu.VMEM((2, 2, 2, tokens, width), bf16),
             pltpu.VMEM((2, 2, 2, tokens, width), bf16),
             pltpu.VMEM((2 * tokens, features), bf16),
@@ -720,8 +703,9 @@
             pltpu.VMEM((groups, tokens), f32),
             pltpu.VMEM((groups // 2 * modes, tokens), f32),
             pltpu.VMEM((tokens, groups // 2 * modes), f32),
-            pltpu.SemaphoreType.DMA((4, 2, 2, n // 2)),
-            pltpu.SemaphoreType.DMA((4, 2, 2, n // 2)),
+            pltpu.VMEM((modes, half), f32),
+            pltpu.SemaphoreType.DMA((4, 2, n // 2)),
+            pltpu.SemaphoreType.DMA((4, 2, n // 2)),
             pltpu.SemaphoreType.DMA((4, 2, n // 2)),
             pltpu.SemaphoreType.DMA((4, 2, n // 2)),
             pltpu.SemaphoreType.DMA((5, 5)),
@@ -746,8 +730,6 @@
         in_weight_b,
         li_rate,
         li_residue,
-        mode_rows,
-        rate_mc,
         out_weight_b,
     )
 

time: 168 us -> 173 us (1.030)
  Pallas kernels: 160 us -> 167 us
    pallas_call x1, Pallas kernels: 160 us -> 167 us  [per_device(): pl.pallas_call(functools.partial(kernel, n, ntp), out_shape=(jax.ShapeDty...]
    unnamed x15 -> x11, local copies, waits for them, and re-layouts: 4.94 us -> 5.53 us
where the time goes in v3:
time: 173 us
  Pallas kernels  167 us (97%)
  local copies, waits for them, and re-layouts  5.53 us (3%)
    pallas_call x1, Pallas kernels, per_device(): pl.pallas_call(functools.partial(kernel, n, ntp), out_shape=(jax.ShapeDty...  167 us
    unnamed x11, local copies, waits for them, and re-layouts  5.53 us

profile of v3, /device:TPU:0, one launch (start us, length us, event | category | flops | bytes accessed | tf_op | source)
XLA Modules:
  0.0 172.9 jit_solution(11238353925416729277)
XLA Ops:
  0.6 0.0 copy-start.2
  0.6 1.4 copy.13.rate
  2.0 0.0 copy-done.2
  2.0 0.7 copy.14.residue
  2.7 166.7 %shard_map.121 = (bf16[256,512]{1,0:T(8,128)(2,1)}, bf16[512,256]{1,0:T(8,128)(2,1)}, bf16[512,256]{1,0:T(8,128)(2,1)}) custom-call(bf16[256,512]{1,0:T(8,128)(2,1)} %hidden.1, f32[1,2048]{1,0:T(1,128)} %bitcast.2, bf16[3,256,512]{2,1,0:T(8,128)(2,1)} %win_a.1, bf16[32,128]{1,0:T(8,128)(2,1)} %mr_filter.1, bf16[512,256]{1,0:T(8,128)(2,1)} %wout_a.1, ...), custom_call_target="tpu_custom_call" | custom-call | flops 5368709120 | bytes 33554432 | tf_op jit(solution)/shard_map/pallas_call | solution.py:669
  169.4 0.0 copy-start.1
  169.4 1.7 copy.18
  171.1 0.0 copy-done.1
  171.1 0.0 copy-start
  171.1 0.7 copy.19
  171.8 0.3 copy-done
  172.2 0.7 copy.20
Async XLA Ops:
  0.6 1.4 copy-start.2
  169.4 1.7 copy-start.1
  171.1 1.0 copy-start

commit v4 on v3

--- a/solution.py
+++ b/solution.py
@@ -129,46 +129,51 @@
             device_id_type=MESH,
         )
 
-    streams = ((win_a, wa), (wout_a, oa), (win_b, wb), (wout_b, ob))
-
-    def slot(stream, owner):
-        buffer = streams[stream][1]
-        if stream in (0, 2):
-            return buffer.at[:, pl.ds(pl.multiple_of(owner * dn, dn), dn), :]
-        return buffer.at[owner]
+    def buffers(stream):
+        return ((win_a, wa, wout_a, oa), (win_b, wb, wout_b, ob))[stream // 4]
+
+    def slot(stream, h, owner):
+        if stream % 4 < 3:
+            rows = pl.ds(pl.multiple_of(owner * dn, dn), dn)
+            return buffers(stream)[1].at[h, stream % 4, rows, :]
+        return buffers(stream)[3].at[h, owner]
 
     def own(stream, h):
-        source = streams[stream][0]
         at = pl.ds(pl.multiple_of(h * channels, channels), channels)
-        return source.at[:, :, at] if stream in (0, 2) else source.at[at, :]
+        if stream % 4 < 3:
+            return buffers(stream)[0].at[stream % 4, :, at]
+        return buffers(stream)[2].at[at, :]
 
     def along(way):
         return (z, 1) if way == 0 else (depth - 1 - z, -1)
 
-    def line_copy(stream, way, step):
+    def line_copy(stream, way, kind, step, first=False):
         zz, d = along(way)
+        h = 1 - lo if kind == 0 else lo
+        owner = (z - d * step) * 2 + y
         return remote(
-            own(stream, lax.rem(z + step, 2)),
-            slot(stream, me),
-            line_send.at[stream, way, step],
-            line_recv.at[stream, way, step],
-            {"ctx": (z + d * step) * 2 + y},
-        )
-
-    def line_arrival(stream, way, step):
+            own(stream, h) if first else slot(stream, h, owner),
+            slot(stream, h, owner),
+            line_send.at[stream, way, kind, step],
+            line_recv.at[stream, way, kind, step],
+            {"ctx": (z + d) * 2 + y},
+        )
+
+    def line_arrival(stream, way, kind, step):
         zz, d = along(way)
-        here = slot(stream, (z - d * step) * 2 + y)
+        h = lo if kind == 0 else 1 - lo
+        here = slot(stream, h, (z - d * (step + 1)) * 2 + y)
         return remote(
             here,
             here,
-            line_send.at[stream, way, step],
-            line_recv.at[stream, way, step],
-            {"ctx": (z - d * step) * 2 + y},
+            line_send.at[stream, way, kind, step],
+            line_recv.at[stream, way, kind, step],
+            {"ctx": (z - d) * 2 + y},
         )
 
     def cross_copy(stream, way, step, side):
         zz, d = along(way)
-        here = slot(stream, (z - d * step) * 2 + side)
+        here = slot(stream, lo, (z - d * step) * 2 + side)
         return remote(
             here, here, cross_send.at[stream, way, step], cross_recv.at[stream, way, step], y_peer
         )
@@ -176,26 +181,22 @@
     def cross_own(stream):
         return remote(
             own(stream, lo),
-            slot(stream, me),
+            slot(stream, lo, me),
             cross_send.at[stream, 0, 0],
             cross_recv.at[stream, 0, 0],
             y_peer,
         )
 
     def start(stream):
-        cross_own(stream).start()
-
-        def body(step, carry):
+        for kind in (1, 0):
             for way in (0, 1):
                 zz, d = along(way)
 
-                @pl.when(zz + step < depth)
+                @pl.when(zz + 1 + kind < depth)
                 def ahead():
-                    line_copy(stream, way, step).start()
-
-            return carry
-
-        lax.fori_loop(1, depth, body, 0)
+                    line_copy(stream, way, kind, 0, True).start()
+
+        cross_own(stream).start()
 
     def pump(stream, low, high):
         def body(step, carry):
@@ -204,13 +205,23 @@
 
                 @pl.when(zz - step >= 0)
                 def arrived():
-                    line_arrival(stream, way, step).wait_recv()
+                    line_arrival(stream, way, 0, step - 1).wait_recv()
+
+                    @pl.when(zz + 2 < depth)
+                    def through():
+                        line_copy(stream, way, 1, step).start()
+
                     cross_copy(stream, way, step, y).start()
 
+                    @pl.when(zz + 1 < depth)
+                    def near():
+                        line_arrival(stream, way, 1, step - 1).wait_recv()
+                        line_copy(stream, way, 0, step).start()
+
             return carry
 
-        if high > low:
-            lax.fori_loop(low, high, body, 0)
+        if min(high, depth) > low:
+            lax.fori_loop(low, min(high, depth), body, 0)
 
     def finish(stream):
         cross_copy(stream, 0, 0, 1 - y).wait_recv()
@@ -235,20 +246,26 @@
             for way in (0, 1):
                 zz, d = along(way)
 
-                @pl.when(zz + step < depth)
-                def ahead():
-                    line_copy(stream, way, step).wait_send()
-
                 @pl.when(zz - step >= 0)
-                def crossed():
-                    cross_copy(stream, way, step, y).wait_send()
+                def passed():
+                    @pl.when(zz + 1 < depth)
+                    def near():
+                        line_copy(stream, way, 0, step).wait_send()
+
+                    @pl.when(zz + 2 < depth)
+                    def through():
+                        line_copy(stream, way, 1, step).wait_send()
+
+                    @pl.when(step > 0)
+                    def crossed():
+                        cross_copy(stream, way, step, y).wait_send()
 
             return carry
 
-        lax.fori_loop(1, depth, body, 0)
+        lax.fori_loop(0, depth, body, 0)
 
     def own_copy(stream):
-        return pltpu.make_async_copy(own(stream, lo), slot(stream, me), local_sems.at[stream])
+        return pltpu.make_async_copy(own(stream, lo), slot(stream, lo, me), local_sems.at[stream])
 
     upper, lower = pl.ds(0, rows2), pl.ds(rows2, rows2)
 
@@ -303,18 +320,16 @@
                 wide = buffer[b, block // 2, block % 2].astype(f32)
                 normed[b * tokens : (b + 1) * tokens, at] = (wide * factor * gain[:, at]).astype(bf16)
 
-    def in_project(weight):
-        def body(k, carry):
-            proj[k] = dot(normed[...], weight[k])
-            return carry
-
-        lax.fori_loop(0, 3, body, 0)
+    def in_project(weight, k):
+        proj[k] = dot(normed[...], weight[lo, k])
+
+    def in_product():
         xin[...] = (proj[0] * proj[2]).astype(bf16)
 
     def out_blocks(buffer, c):
         def body(xx, carry):
             for j in range(width // on):
-                block = dot(gated[...], buffer[(xx * 2 + c) * (width // on) + j]).astype(bf16)
+                block = dot(gated[...], buffer[lo, (xx * 2 + c) * (width // on) + j]).astype(bf16)
                 for b in range(2):
                     part[b, xx, c, :, j * on : (j + 1) * on] = block[b * tokens : (b + 1) * tokens]
             return carry
@@ -408,7 +423,7 @@
         return pl.ds(pl.multiple_of(q * LANES, LANES), LANES)
 
     hbuf[lo, x, core] = hidden[...]
-    for stream in range(4):
+    for stream in range(8):
         own_copy(stream).start()
     pl.semaphore_wait(barrier, (n - 1) + 2)
 
@@ -441,8 +456,13 @@
         return carry
 
     lax.fori_loop(0, groups, build_a, 0)
+    pump(0, 1, 2)
+    start(2)
     gather_second(0, hbuf)
     lax.fori_loop(0, groups, build_b, 0)
+    pump(0, 2, 3)
+    pump(1, 1, 2)
+    start(3)
     gather_third(0, hbuf)
 
     def mode_row(ref):
@@ -464,18 +484,24 @@
     from_start[...] = weight_row * jnp.exp(-rate_row * (position + 1.0))
     to_end[...] = jnp.exp(-rate_row * (tokens - 1.0 - position)).T
 
-    pump(0, 1, 2)
-    pump(1, 1, 2)
+    pump(0, 3, depth)
+    pump(1, 2, 3)
+    pump(2, 1, 2)
+    start(4)
     gather_end(0, hbuf)
     normalize(hbuf, gain_a)
-    pump(0, 2, 3)
-    pump(1, 2, 3)
-    pump(0, 3, depth)
-    start(2)
     pump(1, 3, depth)
+    pump(2, 2, 3)
     finish(0)
-
-    in_project(wa)
+    in_project(wa, 0)
+    pump(3, 1, 2)
+    start(5)
+    finish(1)
+    in_project(wa, 1)
+    pump(2, 3, depth)
+    finish(2)
+    in_project(wa, 2)
+    in_product()
 
     def tail(b):
         return xin.at[pl.ds((b + 1) * tokens - taps, taps), :]
@@ -493,6 +519,9 @@
     )
     for move in halo_moves:
         move.start()
+    pump(3, 2, 3)
+    pump(4, 1, 2)
+    start(6)
     for move in halo_moves:
         move.wait()
 
@@ -523,26 +552,33 @@
     lax.fori_loop(0, tiles, medium_tile, 0)
     product = proj[1] * conv[...]
     gated[...] = product.astype(bf16)
-    finish(1)
+    pump(3, 3, depth)
+    pump(4, 2, 3)
+    pump(5, 1, 2)
+    start(7)
+    finish(3)
     scatter_first(0, oa)
     give_back(0, product)
-    pump(2, 1, 2)
-    start(3)
     scatter_second(0)
     scatter_third(0)
-    pump(2, 2, 3)
+    pump(4, 3, depth)
+    pump(5, 2, 3)
+    pump(6, 1, 2)
     scatter_end(0, hidden, abuf.at[lo, x, core])
     gather_first(1, abuf)
     gather_second(1, abuf)
-    pump(2, 3, depth)
+    pump(5, 3, depth)
+    pump(6, 2, 3)
+    pump(7, 1, 2)
     gather_third(1, abuf)
-    pump(3, 1, 2)
+    pump(6, 3, depth)
+    pump(7, 2, 3)
     gather_end(1, abuf)
     normalize(abuf, gain_b)
-    finish(2)
-
-    pump(3, 2, 3)
-    in_project(wb)
+    for k in (0, 2, 1):
+        finish(4 + k)
+        in_project(wb, k)
+    in_product()
 
     def same_group(shape):
         return lax.div(iota(shape, 0), modes) == lax.div(iota(shape, 1), per)
@@ -574,7 +610,7 @@
         return carry
 
     lax.fori_loop(1, depth, state_start, 0)
-    pump(3, 3, depth)
+    pump(7, 3, depth)
 
     def long_tile(q, carry):
         at = lanes(q)
@@ -621,7 +657,7 @@
             )
     product = proj[1] * conv[...]
     gated[...] = product.astype(bf16)
-    finish(3)
+    finish(7)
     scatter_first(1, ob)
     give_back(1, product)
     scatter_second(1)
@@ -638,7 +674,7 @@
         return carry
 
     lax.fori_loop(1, depth, state_sent, 0)
-    for stream in range(4):
+    for stream in range(8):
         all_sent(stream)
 
 
@@ -676,10 +712,10 @@
         in_specs=[vmem, vmem, anywhere, vmem, anywhere, vmem, anywhere, vmem, vmem, anywhere],
         out_specs=(vmem, vmem, vmem),
         scratch_shapes=[
-            pltpu.VMEM((3, features, half), bf16),
-            pltpu.VMEM((n, half, on), bf16),
-            pltpu.VMEM((3, features, half), bf16),
-            pltpu.VMEM((n, half, on), bf16),
+            pltpu.VMEM((2, 3, features, half), bf16),
+            pltpu.VMEM((2, n, half, on), bf16),
+            pltpu.VMEM((2, 3, features, half), bf16),
+            pltpu.VMEM((2, n, half, on), bf16),
             pltpu.VMEM((2, 2, 2, tokens, width), bf16),
             pltpu.VMEM((2, 2, 2, tokens, width), bf16),
             pltpu.VMEM((2 * tokens, features), bf16),
@@ -704,17 +740,17 @@
             pltpu.VMEM((groups // 2 * modes, tokens), f32),
             pltpu.VMEM((tokens, groups // 2 * modes), f32),
             pltpu.VMEM((modes, half), f32),
-            pltpu.SemaphoreType.DMA((4, 2, n // 2)),
-            pltpu.SemaphoreType.DMA((4, 2, n // 2)),
-            pltpu.SemaphoreType.DMA((4, 2, n // 2)),
-            pltpu.SemaphoreType.DMA((4, 2, n // 2)),
+            pltpu.SemaphoreType.DMA((8, 2, 2, n // 2)),
+            pltpu.SemaphoreType.DMA((8, 2, 2, n // 2)),
+            pltpu.SemaphoreType.DMA((8, 2, n // 2)),
+            pltpu.SemaphoreType.DMA((8, 2, n // 2)),
             pltpu.SemaphoreType.DMA((5, 5)),
             pltpu.SemaphoreType.DMA((5, 5)),
             pltpu.SemaphoreType.DMA((n // 2 - 1,)),
             pltpu.SemaphoreType.DMA((n // 2 - 1,)),
             pltpu.SemaphoreType.DMA((3,)),
             pltpu.SemaphoreType.DMA((3,)),
-            pltpu.SemaphoreType.DMA((4,)),
+            pltpu.SemaphoreType.DMA((8,)),
         ],
         cost_estimate=pl.CostEstimate(flops=flops, bytes_accessed=32 * 1024 * 1024, transcendentals=0),
         compiler_params=pltpu.CompilerParams(

time: 173 us -> 152 us (0.88)
  Pallas kernels: 167 us -> 145 us
    pallas_call x1, Pallas kernels: 167 us -> 145 us  [per_device(): pl.pallas_call(functools.partial(kernel, n, ntp), out_shape=(jax.ShapeDty...]
where the time goes in v4:
time: 152 us; the launch traced here: 151 us
  Pallas kernels  145 us (95%)
  local copies, waits for them, and re-layouts  5.53 us (4%)
    pallas_call x1, Pallas kernels, per_device(): pl.pallas_call(functools.partial(kernel, n, ntp), out_shape=(jax.ShapeDty...  145 us
    unnamed x11, local copies, waits for them, and re-layouts  5.53 us

profile of v4, /device:TPU:0, one launch (start us, length us, event | category | flops | bytes accessed | tf_op | source)
XLA Modules:
  0.0 151.4 jit_solution(16742000450907211865)
XLA Ops:
  0.6 0.0 copy-start.2
  0.6 1.4 copy.13.rate
  2.0 0.0 copy-done.2
  2.0 0.7 copy.14.residue
  2.7 145.2 %shard_map.121 = (bf16[256,512]{1,0:T(8,128)(2,1)}, bf16[512,256]{1,0:T(8,128)(2,1)}, bf16[512,256]{1,0:T(8,128)(2,1)}) custom-call(bf16[256,512]{1,0:T(8,128)(2,1)} %hidden.1, f32[1,2048]{1,0:T(1,128)} %bitcast.2, bf16[3,256,512]{2,1,0:T(8,128)(2,1)} %win_a.1, bf16[32,128]{1,0:T(8,128)(2,1)} %mr_filter.1, bf16[512,256]{1,0:T(8,128)(2,1)} %wout_a.1, ...), custom_call_target="tpu_custom_call" | custom-call | flops 5368709120 | bytes 33554432 | tf_op jit(solution)/shard_map/pallas_call | solution.py:705
  148.0 0.0 copy-start.1
  148.0 1.7 %copy.18 = bf16[256,512]{1,0:T(8,128)(2,1)} copy(bf16[256,512]{1,0:T(8,128)(2,1)} %get-tuple-element.6) | data formatting | bytes 524288
  149.7 0.0 copy-done.1
  149.7 0.0 copy-start
  149.7 0.7 copy.19
  150.4 0.3 copy-done
  150.7 0.7 copy.20
Async XLA Ops:
  0.6 1.4 copy-start.2
  148.0 1.7 %copy-start.1 = (bf16[512,256]{1,0:T(8,128)(2,1)S(1)}, bf16[512,256]{1,0:T(8,128)(2,1)}, u32[]{:S(2)}) copy-start(bf16[512,256]{1,0:T(8,128)(2,1)} %get-tuple-element.7) | copy-start | bytes 786436
  149.7 1.0 copy-start

commit v5 on v4

--- a/solution.py
+++ b/solution.py
@@ -34,8 +34,8 @@
     wout_a,
     gain_b,
     win_b,
-    rate,
-    residue,
+    rate_in,
+    residue_in,
     wout_b,
     mixed,
     gated_a_out,
@@ -68,6 +68,8 @@
     to_end,
     from_start,
     rates_here,
+    rate,
+    residue,
     line_send,
     line_recv,
     cross_send,
@@ -90,7 +92,7 @@
     features = width * ntp
     all_groups, taps = mr_filter.shape
     groups = all_groups // 2
-    modes = rate.shape[1]
+    modes = rate_in.shape[1]
     per = channels // groups
     tile_groups = LANES // per
     tiles = channels // LANES
@@ -422,6 +424,12 @@
     def lanes(q):
         return pl.ds(pl.multiple_of(q * LANES, LANES), LANES)
 
+    filter_copies = (
+        pltpu.make_async_copy(rate_in, rate, local_sems.at[8]),
+        pltpu.make_async_copy(residue_in, residue, local_sems.at[9]),
+    )
+    for copy in filter_copies:
+        copy.start()
     hbuf[lo, x, core] = hidden[...]
     for stream in range(8):
         own_copy(stream).start()
@@ -433,6 +441,8 @@
 
     flip = (lax.rem(iota((taps, taps), 0) + iota((taps, taps), 1), taps) == 0).astype(bf16)
     rows_a[...] = dot(mr_filter[...], flip)
+    for copy in filter_copies:
+        copy.wait()
     lag = lax.rem(tokens - iota((all_groups, tokens), 1), tokens).astype(f32)
     impulse = jnp.zeros((all_groups, tokens), f32)
     for m in range(modes):
@@ -462,7 +472,6 @@
     lax.fori_loop(0, groups, build_b, 0)
     pump(0, 2, 3)
     pump(1, 1, 2)
-    start(3)
     gather_third(0, hbuf)
 
     def mode_row(ref):
@@ -487,11 +496,12 @@
     pump(0, 3, depth)
     pump(1, 2, 3)
     pump(2, 1, 2)
-    start(4)
+    start(3)
     gather_end(0, hbuf)
     normalize(hbuf, gain_a)
     pump(1, 3, depth)
     pump(2, 2, 3)
+    start(4)
     finish(0)
     in_project(wa, 0)
     pump(3, 1, 2)
@@ -522,6 +532,10 @@
     pump(3, 2, 3)
     pump(4, 1, 2)
     start(6)
+    pump(3, 3, depth)
+    pump(4, 2, 3)
+    pump(5, 1, 2)
+    start(7)
     for move in halo_moves:
         move.wait()
 
@@ -552,10 +566,6 @@
     lax.fori_loop(0, tiles, medium_tile, 0)
     product = proj[1] * conv[...]
     gated[...] = product.astype(bf16)
-    pump(3, 3, depth)
-    pump(4, 2, 3)
-    pump(5, 1, 2)
-    start(7)
     finish(3)
     scatter_first(0, oa)
     give_back(0, product)
@@ -709,7 +719,7 @@
             jax.ShapeDtypeStruct((channels, tokens), bf16),
             jax.ShapeDtypeStruct((channels, tokens), bf16),
         ),
-        in_specs=[vmem, vmem, anywhere, vmem, anywhere, vmem, anywhere, vmem, vmem, anywhere],
+        in_specs=[vmem, vmem, anywhere, vmem, anywhere, vmem, anywhere, anywhere, anywhere, anywhere],
         out_specs=(vmem, vmem, vmem),
         scratch_shapes=[
             pltpu.VMEM((2, 3, features, half), bf16),
@@ -740,6 +750,8 @@
             pltpu.VMEM((groups // 2 * modes, tokens), f32),
             pltpu.VMEM((tokens, groups // 2 * modes), f32),
             pltpu.VMEM((modes, half), f32),
+            pltpu.VMEM((groups, modes), f32),
+            pltpu.VMEM((groups, modes), f32),
             pltpu.SemaphoreType.DMA((8, 2, 2, n // 2)),
             pltpu.SemaphoreType.DMA((8, 2, 2, n // 2)),
             pltpu.SemaphoreType.DMA((8, 2, n // 2)),
@@ -750,7 +762,7 @@
             pltpu.SemaphoreType.DMA((n // 2 - 1,)),
             pltpu.SemaphoreType.DMA((3,)),
             pltpu.SemaphoreType.DMA((3,)),
-            pltpu.SemaphoreType.DMA((8,)),
+            pltpu.SemaphoreType.DMA((10,)),
         ],
         cost_estimate=pl.CostEstimate(flops=flops, bytes_accessed=32 * 1024 * 1024, transcendentals=0),
         compiler_params=pltpu.CompilerParams(

time: 152 us -> 153 us (level)
  no operation moved by 1% of the time
where the time goes in v5:
time: 153 us; the launch traced here: 152 us
  Pallas kernels  146 us (95%)
  local copies, waits for them, and re-layouts  5.53 us (4%)
    pallas_call x1, Pallas kernels, per_device(): pl.pallas_call(functools.partial(kernel, n, ntp), out_shape=(jax.ShapeDty...  146 us
    unnamed x11, local copies, waits for them, and re-layouts  5.53 us

profile of v5, /device:TPU:0, one launch (start us, length us, event | category | flops | bytes accessed | tf_op | source)
XLA Modules:
  0.0 152.3 jit_solution(17096280952139246412)
XLA Ops:
  0.6 0.0 copy-start.2
  0.6 1.4 copy.13.rate_in
  2.0 0.0 copy-done.2
  2.0 0.7 copy.14.residue_in
  2.7 146.1 %shard_map.121 = (bf16[256,512]{1,0:T(8,128)(2,1)}, bf16[512,256]{1,0:T(8,128)(2,1)}, bf16[512,256]{1,0:T(8,128)(2,1)}) custom-call(bf16[256,512]{1,0:T(8,128)(2,1)} %hidden.1, f32[1,2048]{1,0:T(1,128)} %bitcast.2, bf16[3,256,512]{2,1,0:T(8,128)(2,1)} %win_a.1, bf16[32,128]{1,0:T(8,128)(2,1)} %mr_filter.1, bf16[512,256]{1,0:T(8,128)(2,1)} %wout_a.1, ...), custom_call_target="tpu_custom_call" | custom-call | flops 5368709120 | bytes 33554432 | tf_op jit(solution)/shard_map/pallas_call | solution.py:715
  148.9 0.0 copy-start.1
  148.9 1.7 %copy.18 = bf16[256,512]{1,0:T(8,128)(2,1)} copy(bf16[256,512]{1,0:T(8,128)(2,1)} %get-tuple-element.6) | data formatting | bytes 524288
  150.6 0.0 copy-done.1
  150.6 0.0 copy-start
  150.6 0.7 copy.19
  151.3 0.3 copy-done
  151.6 0.7 copy.20
Async XLA Ops:
  0.6 1.4 copy-start.2
  148.9 1.7 %copy-start.1 = (bf16[512,256]{1,0:T(8,128)(2,1)S(1)}, bf16[512,256]{1,0:T(8,128)(2,1)}, u32[]{:S(2)}) copy-start(bf16[512,256]{1,0:T(8,128)(2,1)} %get-tuple-element.7) | copy-start | bytes 786436
  150.6 1.0 copy-start
